TPU v7x, 256 devices: a whole 4x4x8 slice. The times are simulated.
256 devices in a mesh: row: 8 (over y, z_lo), col: 32 (over x, z_hi, core).
Axes of the slice: x: 4, y: 4, z: 8 (z_hi: 4, z_lo: 2; z = z_hi * 2 + z_lo), core: 2. Of those that a mesh axis runs over, the one named last changes fastest.
Arguments:
- velocity: bfloat16 [3, 512, 1024, 256], P(None, 'row', 'col'), may hold values from -6 to 6
- adj_temp: bfloat16 [512, 1024, 256], P('row', 'col'), may hold values from -6 to 6
- radial_div: bfloat16 [256, 256], replicated, may hold values from -0.375 to 0.375
- reciprocal_distance: float32 [256], replicated, may hold values from 0.002 to 0.02
- radial_basis: bfloat16 [168, 256, 256], P('row'), may hold values from -0.375 to 0.375
- radial_eig: float32 [168, 256], P('row'), may hold values from 0.5 to 8
- axial_diff: bfloat16 [1024, 1024], replicated, may hold values from -0.1875 to 0.1875
- axial_basis: bfloat16 [1024, 1024], replicated, may hold values from -0.1875 to 0.1875
- axial_eig: float32 [1024], replicated, may hold values from 0.5 to 8
Outputs:
- new_temp: float32 [168, 2, 1024, 256], P('row', None, 'col')
All inputs are finite; a program needn't handle non-finite values.
Results may differ from a plain program's by a relative error of at most 0.0055.
Values may be sent and summed in bfloat16 or wider, within the bound.
No kernel may reach another device: no remote copies, remote signals or barrier semaphores. Data moves between devices by JAX's collectives and lax.ppermute only.
A program may use at most 128 MiB of HBM per device.

v0:
```python
import functools
import math

import jax
import jax.numpy as jnp
from jax import lax
from jax.experimental import pallas as pl
from jax.experimental.pallas import tpu as pltpu
from jax.sharding import PartitionSpec as P

HEAT_OFFSET = 1.0
BF = jnp.bfloat16
F32 = jnp.float32
NT_DIMS = (((1,), (1,)), ((), ()))
VMEM_BYTES = 48 * 1024 * 1024


def azimuth_table(mode_count, angle_count, circle):
    mode_ids = jnp.arange(mode_count, dtype=jnp.int32)
    angle_ids = jnp.arange(angle_count, dtype=jnp.int32)
    phase_index = mode_ids[:, None] * angle_ids[None, :] % circle
    angle_value = phase_index.astype(F32) * (2.0 * math.pi / circle)
    norm_factor = 1.0 / math.sqrt(circle)
    return jnp.concatenate(
        [jnp.cos(angle_value) * norm_factor, -jnp.sin(angle_value) * norm_factor], axis=0
    ).astype(BF)


def vmem():
    return pl.BlockSpec(memory_space=pltpu.VMEM)


def flux_kernel(v_ref, t_ref, d_ref, x_ref):
    t_rows, z_rows, r_rows = t_ref.shape
    temp = t_ref[...].astype(F32)

    def put(field, value):
        value = value.reshape(z_rows, t_rows, r_rows)
        for group in range(4):
            for half in range(2):
                x_ref[group * 2 + half, field] = value[
                    group * 8 : group * 8 + 8, :, half * 128 : half * 128 + 128
                ]

    def flux(c):
        product = v_ref[c].astype(F32) * temp
        return jnp.swapaxes(product, 0, 1).astype(BF)

    put(1, flux(1))
    put(2, flux(2))
    radial = flux(0).reshape(z_rows * t_rows, r_rows)
    turned_temp = jnp.swapaxes(temp, 0, 1).reshape(z_rows * t_rows, r_rows)
    div = lax.dot_general(radial, d_ref[...], NT_DIMS, preferred_element_type=F32)
    put(0, (HEAT_OFFSET * turned_temp + div).astype(BF))


def flux_call(velocity, adj_temp, radial_div):
    _, nt, nz, nr = velocity.shape
    step = 16
    return pl.pallas_call(
        flux_kernel,
        grid=(nt // step,),
        in_specs=[
            pl.BlockSpec((3, step, nz, nr), lambda i: (0, i, 0, 0)),
            pl.BlockSpec((step, nz, nr), lambda i: (i, 0, 0)),
            pl.BlockSpec((nr, nr), lambda i: (0, 0)),
        ],
        out_specs=pl.BlockSpec((8, 3, 8, step, 128), lambda i: (0, 0, 0, i, 0)),
        out_shape=jax.ShapeDtypeStruct((8, 3, 8, nt, 128), BF),
        compiler_params=pltpu.CompilerParams(vmem_limit_bytes=VMEM_BYTES),
        name="flux",
    )(velocity, adj_temp, radial_div)


def spectra_kernel(x_ref, w_ref, recip_ref, y_ref, u_ref):
    rows = w_ref.shape[0]
    modes = rows // 2
    table = w_ref[...]
    mode_id = lax.broadcasted_iota(jnp.int32, (modes, 128), 0).astype(F32)
    scale = mode_id * recip_ref[...]
    scale = jnp.concatenate([scale, scale], axis=0)
    scale = jnp.concatenate([scale, scale], axis=1)
    for z in range(0, 8, 2):

        def transform(field):
            columns = [
                jnp.concatenate([x_ref[s, field, z + k] for s in range(8)], axis=0)
                for k in range(2)
            ]
            return jnp.dot(
                table, jnp.concatenate(columns, axis=1), preferred_element_type=F32
            )

        angular = transform(1).astype(BF).astype(F32)
        turned = jnp.concatenate([-angular[modes:], angular[:modes]], axis=0)
        source = transform(0) + scale * turned
        axial = transform(2)
        for k in range(2):
            lanes = slice(k * 128, k * 128 + 128)
            u_ref[pl.ds(z + k, rows, stride=16), :] = source[:, lanes]
            u_ref[pl.ds(8 + z + k, rows, stride=16), :] = axial[:, lanes]
    block = modes // 8
    for row in range(8):
        for part in range(2):
            first = (part * modes + row * block) * 16
            mine = u_ref[first : first + 16 * 16, :].reshape(16, 16, 128)
            y_ref[row, :, part, 0:16, :] = mine.astype(BF)
            for extra in range(block - 16):
                at = first + (16 + extra) * 16
                for core in range(2):
                    y_ref[row, 2 * extra + part, core, 16:24, :] = u_ref[
                        at + 8 * core : at + 8 * core + 8, :
                    ].astype(BF)
        for chip in range(2 * (block - 16), 16):
            y_ref[row, chip, :, 16:24, :] = jnp.zeros((2, 8, 128), BF)


def spectra_call(fields, table, recip_half):
    return pl.pallas_call(
        spectra_kernel,
        in_specs=[vmem()] * 3,
        out_specs=vmem(),
        out_shape=jax.ShapeDtypeStruct((8, 16, 2, 24, 128), BF),
        scratch_shapes=[pltpu.VMEM((table.shape[0] * 16, 128), F32)],
        compiler_params=pltpu.CompilerParams(vmem_limit_bytes=VMEM_BYTES),
        name="spectra",
    )(fields, table, recip_half)


def axial_solve(hs_ref, hf_ref, low_ref, a_ref, bt_ref, b_ref, r_ref, lam_ref, mu_ref, put):
    nz = hs_ref.shape[0]
    tile = 256
    flux = hf_ref[...].astype(BF)
    for at in range(0, nz, tile):
        combined = hs_ref[at : at + tile, :] + jnp.dot(
            a_ref[at : at + tile, :], flux, preferred_element_type=F32
        )
        low_ref[at : at + tile, :] = combined.astype(BF)
    combined = low_ref[...]
    for at in range(0, nz, tile):
        coefficient = jnp.dot(bt_ref[at : at + tile, :], combined, preferred_element_type=F32)
        coefficient = coefficient / (lam_ref[...] + mu_ref[at : at + tile, :] + HEAT_OFFSET)
        hf_ref[at : at + tile, :] = coefficient
    coefficients = hf_ref[...].astype(BF)
    out_rows = b_ref.shape[0]
    for at in range(0, out_rows, tile):
        returned = jnp.dot(b_ref[at : at + tile, :], coefficients, preferred_element_type=F32)
        value = lax.dot_general(
            returned.astype(BF), r_ref[...], NT_DIMS, preferred_element_type=F32
        )
        put(at, tile, value.astype(BF))


def whole_kernel(y_ref, a_ref, bt_ref, b_ref, r_ref, lam_ref, mu_ref, o_ref, hs_ref, hf_ref, low_ref):
    hs4 = hs_ref.reshape(32, 4, 8, 256)
    hf4 = hf_ref.reshape(32, 4, 8, 256)
    for group in range(4):
        left = jnp.concatenate(
            [y_ref[2 * group + half, :, 0:16, :].reshape(512, 128) for half in range(2)], axis=1
        )
        hat = jnp.dot(left, r_ref[...], preferred_element_type=F32).reshape(32, 2, 8, 256)
        hs4[:, group] = hat[:, 0]
        hf4[:, group] = hat[:, 1]

    def put(at, tile, value):
        o_ref[at // 32 : (at + tile) // 32] = value.reshape(tile // 32, 32, 256)

    axial_solve(hs_ref, hf_ref, low_ref, a_ref, bt_ref, b_ref, r_ref, lam_ref, mu_ref, put)


def shared_kernel(
    core_ref, own_ref, other_ref, whole_ref, a_ref, bt_ref, b_ref, r_ref, lam_ref, mu_ref,
    o_ref, hs_ref, hf_ref, low_ref,
):
    first = core_ref[0] == 0
    hs4 = hs_ref.reshape(32, 4, 8, 256)
    hf4 = hf_ref.reshape(32, 4, 8, 256)
    for group in range(4):

        def hat(ref):
            left = jnp.concatenate(
                [ref[2 * group + half].astype(F32).reshape(256, 128) for half in range(2)], axis=1
            )
            return jnp.dot(
                left.astype(BF), r_ref[...], preferred_element_type=F32
            ).reshape(32, 8, 256)

        own = hat(own_ref)
        other = hat(other_ref)
        hs4[:, group] = jnp.where(first, own, other)
        hf4[:, group] = jnp.where(first, other, own)
    o_ref[:, 0:32, :] = whole_ref[...]

    def put(at, tile, value):
        o_ref[at // 16 : (at + tile) // 16, 32:48, :] = value.reshape(tile // 16, 16, 256)

    axial_solve(hs_ref, hf_ref, low_ref, a_ref, bt_ref, b_ref, r_ref, lam_ref, mu_ref, put)


def solve_scratch():
    return [
        pltpu.VMEM((1024, 256), F32),
        pltpu.VMEM((1024, 256), F32),
        pltpu.VMEM((1024, 256), BF),
    ]


def whole_call(lines, a, bt, b, r, lam, mu):
    return pl.pallas_call(
        whole_kernel,
        in_specs=[vmem()] * 7,
        out_specs=vmem(),
        out_shape=jax.ShapeDtypeStruct((32, 32, 256), BF),
        scratch_shapes=solve_scratch(),
        compiler_params=pltpu.CompilerParams(vmem_limit_bytes=VMEM_BYTES),
        cost_estimate=pl.CostEstimate(flops=4 * 10**9, bytes_accessed=8 * 10**6, transcendentals=0),
        name="whole_pair",
    )(lines, a, bt, b, r, lam, mu)


def shared_call(core, own, other, whole, a, bt, b, r, lam, mu):
    return pl.pallas_call(
        shared_kernel,
        in_specs=[pl.BlockSpec(memory_space=pltpu.SMEM)] + [vmem()] * 9,
        out_specs=vmem(),
        out_shape=jax.ShapeDtypeStruct((32, 48, 256), BF),
        scratch_shapes=solve_scratch(),
        compiler_params=pltpu.CompilerParams(vmem_limit_bytes=VMEM_BYTES),
        name="shared_pair",
    )(core, own, other, whole, a, bt, b, r, lam, mu)


def out_kernel(p_ref, o_ref):
    o_ref[0:16] = p_ref[:, :, 0:32, :].astype(F32)
    for extra in range(o_ref.shape[0] - 16):
        for part in range(2):
            for core in range(2):
                o_ref[16 + extra, part, 16 * core : 16 * core + 16, :] = p_ref[
                    2 * extra + part, core, 32:48, :
                ].astype(F32)


def out_call(pieces, mode_rows):
    return pl.pallas_call(
        out_kernel,
        in_specs=[vmem()],
        out_specs=vmem(),
        out_shape=jax.ShapeDtypeStruct((mode_rows, 2, 32, 256), F32),
        compiler_params=pltpu.CompilerParams(vmem_limit_bytes=VMEM_BYTES),
        name="result",
    )(pieces)


def body(
    velocity,
    adj_temp,
    radial_div,
    reciprocal_distance,
    radial_basis,
    radial_eig,
    axial_diff,
    axial_basis,
    axial_eig,
):
    row_total = lax.axis_size("row")
    col_total = lax.axis_size("col")
    row_place = lax.axis_index("row")
    col_place = lax.axis_index("col")
    chip = col_place // 2
    core = col_place % 2
    mode_rows = radial_basis.shape[0]
    circle = velocity.shape[1] * row_total
    exchange = functools.partial(lax.all_to_all, split_axis=0, concat_axis=0, tiled=True)

    fields = exchange(flux_call(velocity, adj_temp, radial_div), "row")

    table = azimuth_table(mode_rows * row_total, circle, circle)
    recip_half = lax.dynamic_slice_in_dim(reciprocal_distance, (row_place % 2) * 128, 128)
    spectra = spectra_call(fields, table, recip_half[None, :])
    lines = exchange(spectra.reshape(row_total * col_total, 24, 128), ("row", "col"))
    lines = lines.reshape(row_total, col_total, 24, 128)

    own = lines[:, :, 16:24, :]
    other = lax.ppermute(own, "col", [(i, i ^ 1) for i in range(col_total)])
    basis_turned = axial_basis.T
    basis_half = lax.dynamic_index_in_dim(
        axial_basis.reshape(col_total, 2, 16, axial_basis.shape[1]), core, 1, keepdims=False
    ).reshape(col_total * 16, axial_basis.shape[1])
    shared_mode = 16 + jnp.minimum(chip, 2 * (mode_rows - 16) - 1) // 2
    mu = axial_eig[:, None]

    def pick(array, index):
        return lax.dynamic_index_in_dim(array, index, 0, keepdims=False)

    whole = whole_call(
        lines, axial_diff, basis_turned, axial_basis, pick(radial_basis, chip),
        pick(radial_eig, chip)[None, :], mu,
    )
    pieces = shared_call(
        core.reshape(1), own, other, whole, axial_diff, basis_turned, basis_half,
        pick(radial_basis, shared_mode), pick(radial_eig, shared_mode)[None, :], mu,
    )
    pieces = exchange(pieces, "col")
    return out_call(pieces.reshape(16, 2, 48, 256), mode_rows)


def solution(mesh):
    in_specs = (
        P(None, "row", "col", None),
        P("row", "col", None),
        P(),
        P(),
        P("row", None, None),
        P("row", None),
        P(),
        P(),
        P(),
    )
    out_specs = P("row", None, "col", None)
    return jax.shard_map(body, mesh=mesh, in_specs=in_specs, out_specs=out_specs, check_vma=False)
```

profile of v0, /device:TPU:1, one launch (start us, length us, event | category | flops | bytes accessed | tf_op | source)
XLA Modules:
  0.0 155.8 jit_solution(14067783595148609753)
XLA Ops:
  0.0 0.0 copy-start
  0.0 0.0 copy-start.3
  0.0 1.2 copy-done.3
  1.2 0.0 copy-start.4
  1.2 0.9 copy-done.4
  2.1 5.5 %flux.1 = bf16[8,3,8,64,128]{4,3,2,1,0:T(8,128)(2,1)} custom-call(bf16[3,64,32,256]{3,2,1,0:T(8,128)(2,1)} %v_ref.1, bf16[64,32,256]{2,1,0:T(8,128)(2,1)S(1)} %copy-done.3, bf16[256,256]{1,0:T(8,128)(2,1)S(1)} %copy-done.4), custom_call_target="tpu_custom_call" | custom-call | tf_op jit(solution)/shard_map/flux/pallas_call | solution.py:60
  7.6 6.4 %all-to-all-start = ((bf16[8,3,8,64,128]{4,3,2,1,0:T(8,128)(2,1)}), bf16[8,3,8,64,128]{4,3,2,1,0:T(8,128)(2,1)S(1)}, u32[]{:S(2)}, u32[]{:S(2)}) async-start(bf16[8,3,8,64,128]{4,3,2,1,0:T(8,128)(2,1)} %flux.1), calls=%async_computation | async-start | bytes 6291456 | tf_op jit(solution)/shard_map/all_to_all | solution.py:275
  14.0 0.0 copy-done
  14.0 0.1 dynamic-slice_bitcast_fusion.2.recip_ref
  14.1 1.4 multiply_convert_fusion
  15.6 35.7 %all-to-all-done.x_ref = bf16[8,3,8,64,128]{4,3,2,1,0:T(8,128)(2,1)S(1)} async-done(((bf16[8,3,8,64,128]{4,3,2,1,0:T(8,128)(2,1)}), bf16[8,3,8,64,128]{4,3,2,1,0:T(8,128)(2,1)S(1)}, u32[]{:S(2)}, u32[]{:S(2)}) %all-to-all-start) | async-done | bytes 3145760 | tf_op jit(solution)/shard_map/all_to_all | solution.py:275
  51.3 2.0 %spectra.1 = bf16[8,16,2,24,128]{4,3,2,1,0:T(8,128)(2,1)S(1)} custom-call(bf16[8,3,8,64,128]{4,3,2,1,0:T(8,128)(2,1)S(1)} %all-to-all-done.x_ref, bf16[336,512]{1,0:T(8,128)(2,1)S(1)} %pad_maximum_fusion.w_ref, f32[1,128]{1,0:T(1,128)S(1)} %dynamic-slice_bitcast_fusion.2.recip_ref), custom_call_target="tpu_custom_call" | custom-call | tf_op jit(solution)/shard_map/spectra/pallas_call | solution.py:119
  53.3 0.0 copy-start.1
  53.3 1.2 copy-done.1
  54.4 13.4 %all-to-all-start.1 = ((bf16[256,24,128]{2,1,0:T(8,128)(2,1)}), bf16[256,24,128]{2,1,0:T(8,128)(2,1)S(1)}, u32[]{:S(2)}, u32[]{:S(2)}) async-start(bf16[256,24,128]{2,1,0:T(8,128)(2,1)} %bitcast.16), calls=%async_computation.1 | async-start | bytes 3145728 | tf_op jit(solution)/shard_map/all_to_all | solution.py:280
  67.9 1.0 dynamic-slice_bitcast_fusion
  68.9 40.9 %all-to-all-done.1 = bf16[256,24,128]{2,1,0:T(8,128)(2,1)S(1)} async-done(((bf16[256,24,128]{2,1,0:T(8,128)(2,1)}), bf16[256,24,128]{2,1,0:T(8,128)(2,1)S(1)}, u32[]{:S(2)}, u32[]{:S(2)}) %all-to-all-start.1) | async-done | bytes 1572896 | tf_op jit(solution)/shard_map/all_to_all | solution.py:280
  109.8 0.1 slice.4.own_ref
  109.9 1.6 %collective-permute-start = (bf16[8,32,8,128]{3,2,1,0:T(8,128)(2,1)S(1)}, bf16[8,32,8,128]{3,2,1,0:T(8,128)(2,1)S(1)}, u32[]{:S(2)}, u32[]{:S(2)}) collective-permute-start(bf16[8,32,8,128]{3,2,1,0:T(8,128)(2,1)S(1)} %slice.4.own_ref), channel_id=1, source_target_pairs={{0,1},{1,0},{2,3},{3,2},{4,5},{5,4},{6,7},{7,6},{8,9},{9,8},{10,11... | collective-permute-start | bytes 1572872 | tf_op jit(solution)/shard_map/ppermute | solution.py:284
  111.5 0.7 constant_dynamic-slice_fusion
  112.2 0.0 copy-start.5
  112.2 4.0 %copy.12 = bf16[1024,1024]{0,1:T(8,128)(2,1)} copy(bf16[1024,1024]{1,0:T(8,128)(2,1)} %b_ref.1) | data formatting | bytes 4194304 | tf_op args[7]
  116.1 0.0 copy-done.5
  116.1 0.2 copy.13.mu_ref
  116.4 0.0 copy-start.2
  116.4 1.5 constant_dynamic-slice_fusion.1
  117.9 0.4 copy-done.2
  118.3 5.3 %whole_pair.1.whole_ref = bf16[32,32,256]{2,1,0:T(8,128)(2,1)S(1)} custom-call(bf16[8,32,24,128]{3,2,1,0:T(8,128)(2,1)S(1)} %bitcast.20, bf16[1024,1024]{1,0:T(8,128)(2,1)S(1)} %copy-done.2, bf16[1024,1024]{1,0:T(8,128)(2,1)} %bitcast.21, bf16[1024,1024]{1,0:T(8,128)(2,1)} %b_ref.1, bf16[256,256]{1,0:T(8,128)(2,1)S(1)} %get-tuple-element.6.r_ref, ...), custom_call_target="tpu_custom_call" | custom-call | flops 4000000000 | bytes 8000000 | tf_op jit(solution)/shard_map/whole_pair/pallas_call | solution.py:209
  123.6 0.0 collective-permute-done.other_ref
  123.7 4.1 %shared_pair.1 = bf16[32,48,256]{2,1,0:T(8,128)(2,1)S(1)} custom-call(s32[1]{0:T(128)} %bitcast.core_ref, bf16[8,32,8,128]{3,2,1,0:T(8,128)(2,1)S(1)} %slice.4.own_ref, bf16[8,32,8,128]{3,2,1,0:T(8,128)(2,1)S(1)} %collective-permute-done.other_ref, bf16[32,32,256]{2,1,0:T(8,128)(2,1)S(1)} %whole_pair.1.whole_ref, bf16[1024,1024]{1,0:T(8,128)(2,1)S(1)} %copy-done.2, ...), custom_call_target="tpu_custom_call" | custom-call | tf_op jit(solution)/shard_map/shared_pair/pallas_call | solution.py:222
  127.7 26.9 %all_to_all.15 = bf16[32,48,256]{2,1,0:T(8,128)(2,1)S(1)} all-to-all(bf16[32,48,256]{2,1,0:T(8,128)(2,1)S(1)} %shared_pair.1), channel_id=1, replica_groups=mesh['row'=8,'col'=32] {'col'}, dimensions={0} | all-to-all | bytes 1572864 | tf_op jit(solution)/shard_map/all_to_all | solution.py:303
  154.6 1.2 result.1
  (1 shorter events, 0.0 us)
Async XLA Ops:
  0.0 14.0 %copy-start = (f32[256]{0:T(256)S(1)}, f32[256]{0:T(256)}, u32[]{:S(2)}) copy-start(f32[256]{0:T(256)} %param.12) | copy-start | bytes 3076
  0.0 1.2 copy-start.3
  1.2 0.9 copy-start.4
  7.6 43.7 %all-to-all-start = ((bf16[8,3,8,64,128]{4,3,2,1,0:T(8,128)(2,1)}), bf16[8,3,8,64,128]{4,3,2,1,0:T(8,128)(2,1)S(1)}, u32[]{:S(2)}, u32[]{:S(2)}) async-start(bf16[8,3,8,64,128]{4,3,2,1,0:T(8,128)(2,1)} %flux.1), calls=%async_computation | async-start | bytes 6291456 | tf_op jit(solution)/shard_map/all_to_all | solution.py:275
  53.3 1.2 copy-start.1
  54.4 55.3 %all-to-all-start.1 = ((bf16[256,24,128]{2,1,0:T(8,128)(2,1)}), bf16[256,24,128]{2,1,0:T(8,128)(2,1)S(1)}, u32[]{:S(2)}, u32[]{:S(2)}) async-start(bf16[256,24,128]{2,1,0:T(8,128)(2,1)} %bitcast.16), calls=%async_computation.1 | async-start | bytes 3145728 | tf_op jit(solution)/shard_map/all_to_all | solution.py:280
  109.9 13.8 %collective-permute-start = (bf16[8,32,8,128]{3,2,1,0:T(8,128)(2,1)S(1)}, bf16[8,32,8,128]{3,2,1,0:T(8,128)(2,1)S(1)}, u32[]{:S(2)}, u32[]{:S(2)}) collective-permute-start(bf16[8,32,8,128]{3,2,1,0:T(8,128)(2,1)S(1)} %slice.4.own_ref), channel_id=1, source_target_pairs={{0,1},{1,0},{2,3},{3,2},{4,5},{5,4},{6,7},{7,6},{8,9},{9,8},{10,11... | collective-permute-start | bytes 1572872 | tf_op jit(solution)/shard_map/ppermute | solution.py:284
  112.2 4.0 %copy-start.5 = (f32[1024]{0:T(1024)S(1)}, f32[1024]{0:T(1024)}, u32[]{:S(2)}) copy-start(f32[1024]{0:T(1024)} %param.17) | copy-start | bytes 12292
  116.4 1.9 %copy-start.2 = (bf16[1024,1024]{1,0:T(8,128)(2,1)S(1)}, bf16[1024,1024]{1,0:T(8,128)(2,1)}, u32[]{:S(2)}) copy-start(bf16[1024,1024]{1,0:T(8,128)(2,1)} %a_ref.3) | copy-start | bytes 6291460
where the time goes:
time: 156 us
  waiting for transfers between devices  76.7 us (49%)
  blocking collectives  26.9 us (17%)
  starting transfers between devices  21.3 us (14%)
  Pallas kernels  18 us (12%)
  local copies, waits for them, and re-layouts  11.3 us (7%)
    all_to_all x1, waiting for transfers between devices, body(): exchange(spectra.reshape(row_total * col_total, 24, 128), ('row', 'col'))  40.9 us
    all_to_all x1, waiting for transfers between devices, body(): fields = exchange(flux_call(velocity, adj_temp, radial_div), 'row')  35.7 us
    all_to_all x1, blocking collectives, body(): pieces = exchange(pieces, 'col')  26.9 us
    all_to_all x1, starting transfers between devices, body(): exchange(spectra.reshape(row_total * col_total, 24, 128), ('row', 'col'))  13.4 us
    unnamed x13, local copies, waits for them, and re-layouts  7.67 us
    all_to_all x1, starting transfers between devices, body(): fields = exchange(flux_call(velocity, adj_temp, radial_div), 'row')  6.37 us
    pallas_call x1, Pallas kernels, flux_call(): pl.pallas_call(flux_kernel, grid=(nt // step,), in_specs=[pl.BlockSpec((3...  5.5 us
    pallas_call x1, Pallas kernels, whole_call(): pl.pallas_call(whole_kernel, in_specs=[vmem()] * 7, out_specs=vmem(), out...  5.35 us
  transfers between devices with their start and end apart: 3, of which 2 were waited for; matrix products, arithmetic and copies ran while one was open for 6% of the time, Pallas kernels for 3%

commit v1 on v0

--- a/solution.py
+++ b/solution.py
@@ -12,7 +12,9 @@
 BF = jnp.bfloat16
 F32 = jnp.float32
 NT_DIMS = (((1,), (1,)), ((), ()))
-VMEM_BYTES = 48 * 1024 * 1024
+MIB = 1024 * 1024
+SPECTRA_LIMIT = 24 * MIB
+SOLVE_LIMIT = 24 * MIB
 
 
 def azimuth_table(mode_count, angle_count, circle):
@@ -38,7 +40,7 @@
         value = value.reshape(z_rows, t_rows, r_rows)
         for group in range(4):
             for half in range(2):
-                x_ref[group * 2 + half, field] = value[
+                x_ref[group * 2 + half, field, 0] = value[
                     group * 8 : group * 8 + 8, :, half * 128 : half * 128 + 128
                 ]
 
@@ -56,7 +58,7 @@
 
 def flux_call(velocity, adj_temp, radial_div):
     _, nt, nz, nr = velocity.shape
-    step = 16
+    step = 32
     return pl.pallas_call(
         flux_kernel,
         grid=(nt // step,),
@@ -65,14 +67,15 @@
             pl.BlockSpec((step, nz, nr), lambda i: (i, 0, 0)),
             pl.BlockSpec((nr, nr), lambda i: (0, 0)),
         ],
-        out_specs=pl.BlockSpec((8, 3, 8, step, 128), lambda i: (0, 0, 0, i, 0)),
-        out_shape=jax.ShapeDtypeStruct((8, 3, 8, nt, 128), BF),
-        compiler_params=pltpu.CompilerParams(vmem_limit_bytes=VMEM_BYTES),
+        out_specs=pl.BlockSpec((8, 3, 1, 8, step, 128), lambda i: (0, 0, i, 0, 0, 0)),
+        out_shape=jax.ShapeDtypeStruct((8, 3, nt // step, 8, step, 128), BF),
+        compiler_params=pltpu.CompilerParams(vmem_limit_bytes=60 * MIB),
         name="flux",
     )(velocity, adj_temp, radial_div)
 
 
-def spectra_kernel(x_ref, w_ref, recip_ref, y_ref, u_ref):
+def spectra_kernel(x_ref, w_ref, recip_ref, *rest):
+    y_ref, u_ref = rest[-2:]
     rows = w_ref.shape[0]
     modes = rows // 2
     table = w_ref[...]
@@ -80,25 +83,32 @@
     scale = mode_id * recip_ref[...]
     scale = jnp.concatenate([scale, scale], axis=0)
     scale = jnp.concatenate([scale, scale], axis=1)
-    for z in range(0, 8, 2):
-
-        def transform(field):
-            columns = [
-                jnp.concatenate([x_ref[s, field, z + k] for s in range(8)], axis=0)
-                for k in range(2)
-            ]
-            return jnp.dot(
-                table, jnp.concatenate(columns, axis=1), preferred_element_type=F32
+    z = 2 * pl.program_id(0)
+
+    def transform(field):
+        columns = [
+            jnp.concatenate(
+                [x_ref[s, field, h, k] for s in range(8) for h in range(2)], axis=0
             )
-
-        angular = transform(1).astype(BF).astype(F32)
-        turned = jnp.concatenate([-angular[modes:], angular[:modes]], axis=0)
-        source = transform(0) + scale * turned
-        axial = transform(2)
-        for k in range(2):
-            lanes = slice(k * 128, k * 128 + 128)
-            u_ref[pl.ds(z + k, rows, stride=16), :] = source[:, lanes]
-            u_ref[pl.ds(8 + z + k, rows, stride=16), :] = axial[:, lanes]
+            for k in range(2)
+        ]
+        return jnp.dot(table, jnp.concatenate(columns, axis=1), preferred_element_type=F32)
+
+    angular = transform(1).astype(BF).astype(F32)
+    turned = jnp.concatenate([-angular[modes:], angular[:modes]], axis=0)
+    source = transform(0) + scale * turned
+    axial = transform(2)
+    for k in range(2):
+        lanes = slice(k * 128, k * 128 + 128)
+        u_ref[pl.ds(z + k, rows, stride=16), :] = source[:, lanes]
+        u_ref[pl.ds(8 + z + k, rows, stride=16), :] = axial[:, lanes]
+
+    @pl.when(pl.program_id(0) == pl.num_programs(0) - 1)
+    def _():
+        write_messages(u_ref, y_ref, modes)
+
+
+def write_messages(u_ref, y_ref, modes):
     block = modes // 8
     for row in range(8):
         for part in range(2):
@@ -115,22 +125,26 @@
             y_ref[row, chip, :, 16:24, :] = jnp.zeros((2, 8, 128), BF)
 
 
-def spectra_call(fields, table, recip_half):
+def spectra_call(fields, table, recip_half, later):
     return pl.pallas_call(
         spectra_kernel,
-        in_specs=[vmem()] * 3,
+        grid=(4,),
+        in_specs=[pl.BlockSpec((8, 3, 2, 2, 32, 128), lambda i: (0, 0, 0, i, 0, 0))]
+        + [vmem()] * 2
+        + [pl.BlockSpec(memory_space=pl.ANY)] * len(later),
         out_specs=vmem(),
         out_shape=jax.ShapeDtypeStruct((8, 16, 2, 24, 128), BF),
         scratch_shapes=[pltpu.VMEM((table.shape[0] * 16, 128), F32)],
-        compiler_params=pltpu.CompilerParams(vmem_limit_bytes=VMEM_BYTES),
+        compiler_params=pltpu.CompilerParams(vmem_limit_bytes=SPECTRA_LIMIT),
         name="spectra",
-    )(fields, table, recip_half)
+    )(fields, table, recip_half, *later)
 
 
 def axial_solve(hs_ref, hf_ref, low_ref, a_ref, bt_ref, b_ref, r_ref, lam_ref, mu_ref, put):
     nz = hs_ref.shape[0]
     tile = 256
     flux = hf_ref[...].astype(BF)
+    shift = jnp.transpose(jnp.broadcast_to(mu_ref[...], (8, nz)))[:, 0:1] + HEAT_OFFSET
     for at in range(0, nz, tile):
         combined = hs_ref[at : at + tile, :] + jnp.dot(
             a_ref[at : at + tile, :], flux, preferred_element_type=F32
@@ -139,7 +153,7 @@
     combined = low_ref[...]
     for at in range(0, nz, tile):
         coefficient = jnp.dot(bt_ref[at : at + tile, :], combined, preferred_element_type=F32)
-        coefficient = coefficient / (lam_ref[...] + mu_ref[at : at + tile, :] + HEAT_OFFSET)
+        coefficient = coefficient / (lam_ref[...] + shift[at : at + tile, :])
         hf_ref[at : at + tile, :] = coefficient
     coefficients = hf_ref[...].astype(BF)
     out_rows = b_ref.shape[0]
@@ -212,7 +226,7 @@
         out_specs=vmem(),
         out_shape=jax.ShapeDtypeStruct((32, 32, 256), BF),
         scratch_shapes=solve_scratch(),
-        compiler_params=pltpu.CompilerParams(vmem_limit_bytes=VMEM_BYTES),
+        compiler_params=pltpu.CompilerParams(vmem_limit_bytes=SOLVE_LIMIT),
         cost_estimate=pl.CostEstimate(flops=4 * 10**9, bytes_accessed=8 * 10**6, transcendentals=0),
         name="whole_pair",
     )(lines, a, bt, b, r, lam, mu)
@@ -225,7 +239,7 @@
         out_specs=vmem(),
         out_shape=jax.ShapeDtypeStruct((32, 48, 256), BF),
         scratch_shapes=solve_scratch(),
-        compiler_params=pltpu.CompilerParams(vmem_limit_bytes=VMEM_BYTES),
+        compiler_params=pltpu.CompilerParams(vmem_limit_bytes=SOLVE_LIMIT),
         name="shared_pair",
     )(core, own, other, whole, a, bt, b, r, lam, mu)
 
@@ -246,7 +260,7 @@
         in_specs=[vmem()],
         out_specs=vmem(),
         out_shape=jax.ShapeDtypeStruct((mode_rows, 2, 32, 256), F32),
-        compiler_params=pltpu.CompilerParams(vmem_limit_bytes=VMEM_BYTES),
+        compiler_params=pltpu.CompilerParams(vmem_limit_bytes=SOLVE_LIMIT),
         name="result",
     )(pieces)
 
@@ -274,31 +288,35 @@
 
     fields = exchange(flux_call(velocity, adj_temp, radial_div), "row")
 
+    def pick(array, index):
+        return lax.dynamic_index_in_dim(array, index, 0, keepdims=False)
+
     table = azimuth_table(mode_rows * row_total, circle, circle)
     recip_half = lax.dynamic_slice_in_dim(reciprocal_distance, (row_place % 2) * 128, 128)
-    spectra = spectra_call(fields, table, recip_half[None, :])
+    basis_turned = axial_basis.T
+    basis_half = pick(
+        axial_basis.reshape(col_total, 2, 16, axial_basis.shape[1]).swapaxes(0, 1), core
+    ).reshape(col_total * 16, axial_basis.shape[1])
+    shared_mode = 16 + jnp.minimum(chip, 2 * (mode_rows - 16) - 1) // 2
+    mu = axial_eig[None, :]
+    whole_basis, shared_basis = pick(radial_basis, chip), pick(radial_basis, shared_mode)
+    whole_eig, shared_eig = pick(radial_eig, chip)[None, :], pick(radial_eig, shared_mode)[None, :]
+
+    later = [whole_basis, shared_basis, whole_eig, shared_eig]
+    fields, later = lax.optimization_barrier((fields, later))
+    whole_basis, shared_basis, whole_eig, shared_eig = later
+    spectra = spectra_call(fields, table, recip_half[None, :], [basis_turned, basis_half])
     lines = exchange(spectra.reshape(row_total * col_total, 24, 128), ("row", "col"))
     lines = lines.reshape(row_total, col_total, 24, 128)
 
     own = lines[:, :, 16:24, :]
     other = lax.ppermute(own, "col", [(i, i ^ 1) for i in range(col_total)])
-    basis_turned = axial_basis.T
-    basis_half = lax.dynamic_index_in_dim(
-        axial_basis.reshape(col_total, 2, 16, axial_basis.shape[1]), core, 1, keepdims=False
-    ).reshape(col_total * 16, axial_basis.shape[1])
-    shared_mode = 16 + jnp.minimum(chip, 2 * (mode_rows - 16) - 1) // 2
-    mu = axial_eig[:, None]
-
-    def pick(array, index):
-        return lax.dynamic_index_in_dim(array, index, 0, keepdims=False)
-
     whole = whole_call(
-        lines, axial_diff, basis_turned, axial_basis, pick(radial_basis, chip),
-        pick(radial_eig, chip)[None, :], mu,
+        lines, axial_diff, basis_turned, axial_basis, whole_basis, whole_eig, mu
     )
     pieces = shared_call(
         core.reshape(1), own, other, whole, axial_diff, basis_turned, basis_half,
-        pick(radial_basis, shared_mode), pick(radial_eig, shared_mode)[None, :], mu,
+        shared_basis, shared_eig, mu,
     )
     pieces = exchange(pieces, "col")
     return out_call(pieces.reshape(16, 2, 48, 256), mode_rows)

time: 156 us -> 144 us (0.923)
  blocking collectives: 26.9 us -> 82.3 us
  waiting for transfers between devices: 76.7 us -> 29 us
  starting transfers between devices: 21.3 us -> 7.95 us
  local copies, waits for them, and re-layouts: 11.3 us -> 6.75 us
  Pallas kernels: 18 us -> 16.1 us
    all_to_all x0 -> x1, blocking collectives: none -> 55.4 us  [body(): exchange(spectra.reshape(row_total * col_total, 24, 128), ('row', 'col'))]
    all_to_all x1 -> x0, waiting for transfers between devices: 40.9 us -> none  [body(): exchange(spectra.reshape(row_total * col_total, 24, 128), ('row', 'col'))]
    all_to_all x1 -> x0, starting transfers between devices: 13.4 us -> none  [body(): exchange(spectra.reshape(row_total * col_total, 24, 128), ('row', 'col'))]
    all_to_all x1, waiting for transfers between devices: 35.7 us -> 29 us  [body(): fields = exchange(flux_call(velocity, adj_temp, radial_div), 'row')]
    unnamed x13, local copies, waits for them, and re-layouts: 7.67 us -> 2.89 us
    pallas_call x1, Pallas kernels: 1.95 us -> 4.24 us  [spectra_call(): pl.pallas_call(spectra_kernel, grid=(4,), in_specs=[pl.BlockSpec((8, 3, 2...]
    pallas_call x1, Pallas kernels: 5.35 us -> 3.15 us  [whole_call(): pl.pallas_call(whole_kernel, in_specs=[vmem()] * 7, out_specs=vmem(), out...]
    pallas_call x1, Pallas kernels: 4.08 us -> 2.48 us  [shared_call(): pl.pallas_call(shared_kernel, in_specs=[pl.BlockSpec(memory_space=pltpu.S...]
  transfers between devices with their start and end apart: 3 -> 2, of which waited for: 2 -> 1; matrix products, arithmetic and copies ran while one was open for 6% -> 6% of each run, Pallas kernels for 3% -> 2%
where the time goes in v1:
time: 144 us
  blocking collectives  82.3 us (57%)
  waiting for transfers between devices  29 us (20%)
  Pallas kernels  16.1 us (11%)
  starting transfers between devices  7.95 us (6%)
  local copies, waits for them, and re-layouts  6.75 us (5%)
  other arithmetic  1.46 us (1%)
    all_to_all x1, blocking collectives, body(): exchange(spectra.reshape(row_total * col_total, 24, 128), ('row', 'col'))  55.4 us
    all_to_all x1, waiting for transfers between devices, body(): fields = exchange(flux_call(velocity, adj_temp, radial_div), 'row')  29 us
    all_to_all x1, blocking collectives, body(): pieces = exchange(pieces, 'col')  26.9 us
    all_to_all x1, starting transfers between devices, body(): fields = exchange(flux_call(velocity, adj_temp, radial_div), 'row')  6.37 us
    pallas_call x1, Pallas kernels, flux_call(): pl.pallas_call(flux_kernel, grid=(nt // step,), in_specs=[pl.BlockSpec((3...  5.09 us
    pallas_call x1, Pallas kernels, spectra_call(): pl.pallas_call(spectra_kernel, grid=(4,), in_specs=[pl.BlockSpec((8, 3, 2...  4.24 us
    pallas_call x1, Pallas kernels, whole_call(): pl.pallas_call(whole_kernel, in_specs=[vmem()] * 7, out_specs=vmem(), out...  3.15 us
    unnamed x13, local copies, waits for them, and re-layouts  2.89 us
  transfers between devices with their start and end apart: 2, of which 1 were waited for; matrix products, arithmetic and copies ran while one was open for 6% of the time, Pallas kernels for 2%

profile of v1, /device:TPU:1, one launch (start us, length us, event | category | flops | bytes accessed | tf_op | source)
XLA Modules:
  0.0 143.7 jit_solution(7610926377823932896)
XLA Ops:
  0.0 0.0 copy-start
  0.0 5.1 %flux.1 = bf16[8,3,2,8,32,128]{5,4,3,2,1,0:T(8,128)(2,1)} custom-call(bf16[3,64,32,256]{3,2,1,0:T(8,128)(2,1)} %v_ref.1, bf16[64,32,256]{2,1,0:T(8,128)(2,1)} %t_ref.1, bf16[256,256]{1,0:T(8,128)(2,1)} %d_ref.1), custom_call_target="tpu_custom_call" | custom-call | tf_op jit(solution)/shard_map/flux/pallas_call | solution.py:62
  5.1 6.4 %all-to-all-start = ((bf16[8,3,2,8,32,128]{5,4,3,2,1,0:T(8,128)(2,1)}), bf16[8,3,2,8,32,128]{5,4,3,2,1,0:T(8,128)(2,1)}, u32[]{:S(2)}, u32[]{:S(2)}) async-start(bf16[8,3,2,8,32,128]{5,4,3,2,1,0:T(8,128)(2,1)} %flux.1), calls=%async_computation | async-start | bytes 6291456 | tf_op jit(solution)/shard_map/all_to_all | solution.py:289
  11.5 2.9 %copy.10 = bf16[1024,1024]{0,1:T(8,128)(2,1)S(1)} copy(bf16[1024,1024]{1,0:T(8,128)(2,1)} %b_ref.1) | data formatting | bytes 4194304 | tf_op args[7]
  14.4 0.0 copy-done
  14.4 0.1 dynamic-slice_bitcast_fusion.2.recip_ref
  14.4 0.7 constant_dynamic-slice_fusion.1
  15.2 1.7 %dynamic-slice_bitcast_fusion = (bf16[256,256]{1,0:T(8,128)(2,1)}, bf16[256,256]{1,0:T(8,128)(2,1)}) fusion(bf16[21,256,256]{2,1,0:T(8,128)(2,1)} %param.13, s32[]{:T(128)S(6)} %select_n.47, s32[]{:T(128)S(6)} %select_n.45), kind=kLoop, calls=%fused_computation.12 | loop fusion | bytes 524296 | tf_op jit(solution)/shard_map/jit(dynamic_index_in_dim)/squeeze | solution.py:292
  16.8 1.4 multiply_convert_fusion
  18.3 1.3 constant_dynamic-slice_fusion
  19.6 29.0 %all-to-all-done.x_ref = bf16[8,3,2,8,32,128]{5,4,3,2,1,0:T(8,128)(2,1)} async-done(((bf16[8,3,2,8,32,128]{5,4,3,2,1,0:T(8,128)(2,1)}), bf16[8,3,2,8,32,128]{5,4,3,2,1,0:T(8,128)(2,1)}, u32[]{:S(2)}, u32[]{:S(2)}) %all-to-all-start) | async-done | bytes 3145760 | tf_op jit(solution)/shard_map/all_to_all | solution.py:289
  48.6 0.0 copy-start.4
  48.6 0.0 copy-start.5
  48.6 4.2 %spectra.1 = bf16[8,16,2,24,128]{4,3,2,1,0:T(8,128)(2,1)S(1)} custom-call(bf16[8,3,2,8,32,128]{5,4,3,2,1,0:T(8,128)(2,1)} %all-to-all-done.x_ref, bf16[336,512]{1,0:T(8,128)(2,1)S(1)} %pad_maximum_fusion.w_ref, f32[1,128]{1,0:T(1,128)S(1)} %dynamic-slice_bitcast_fusion.2.recip_ref, bf16[1024,1024]{1,0:T(8,128)(2,1)S(1)} %bitcast.16, ...), custom_call_target="tpu_custom_call" | custom-call | tf_op jit(solution)/shard_map/spectra/pallas_call | solution.py:129
  52.8 0.0 copy-start.1
  52.8 0.0 copy-start.2
  52.9 55.4 %all_to_all.15 = bf16[256,24,128]{2,1,0:T(8,128)(2,1)S(1)} all-to-all(bf16[256,24,128]{2,1,0:T(8,128)(2,1)S(1)} %bitcast.21), channel_id=1, replica_groups=mesh['row'=8,'col'=32] {'row','col'}, dimensions={0} | all-to-all | bytes 3145728 | tf_op jit(solution)/shard_map/all_to_all | solution.py:309
  108.3 0.1 slice.4.own_ref
  108.4 1.6 %collective-permute-start = (bf16[8,32,8,128]{3,2,1,0:T(8,128)(2,1)S(1)}, bf16[8,32,8,128]{3,2,1,0:T(8,128)(2,1)S(1)}, u32[]{:S(2)}, u32[]{:S(2)}) collective-permute-start(bf16[8,32,8,128]{3,2,1,0:T(8,128)(2,1)S(1)} %slice.4.own_ref), channel_id=1, source_target_pairs={{0,1},{1,0},{2,3},{3,2},{4,5},{5,4},{6,7},{7,6},{8,9},{9,8},{10,11... | collective-permute-start | bytes 1572872 | tf_op jit(solution)/shard_map/ppermute | solution.py:313
  110.0 0.0 copy-done.4
  110.0 0.0 copy-done.5
  110.0 0.0 copy-done.1
  110.0 0.0 copy-done.2
  110.0 0.0 copy-start.3
  110.0 3.1 %whole_pair.1.whole_ref = bf16[32,32,256]{2,1,0:T(8,128)(2,1)S(1)} custom-call(bf16[8,32,24,128]{3,2,1,0:T(8,128)(2,1)S(1)} %bitcast.25, bf16[1024,1024]{1,0:T(8,128)(2,1)S(1)} %copy-done.2, bf16[1024,1024]{1,0:T(8,128)(2,1)S(1)} %bitcast.17, bf16[1024,1024]{1,0:T(8,128)(2,1)S(1)} %copy-done.1, bf16[256,256]{1,0:T(8,128)(2,1)S(1)} %copy-done.4, ...), custom_call_target="tpu_custom_call" | custom-call | flops 4000000000 | bytes 8000000 | tf_op jit(solution)/shard_map/whole_pair/pallas_call | solution.py:223
  113.1 0.0 collective-permute-done.other_ref
  113.2 0.0 copy-done.3
  113.2 2.5 %shared_pair.1 = bf16[32,48,256]{2,1,0:T(8,128)(2,1)S(1)} custom-call(s32[1]{0:T(128)} %bitcast.core_ref, bf16[8,32,8,128]{3,2,1,0:T(8,128)(2,1)S(1)} %slice.4.own_ref, bf16[8,32,8,128]{3,2,1,0:T(8,128)(2,1)S(1)} %collective-permute-done.other_ref, bf16[32,32,256]{2,1,0:T(8,128)(2,1)S(1)} %whole_pair.1.whole_ref, bf16[1024,1024]{1,0:T(8,128)(2,1)S(1)} %copy-done.2, ...), custom_call_target="tpu_custom_call" | custom-call | tf_op jit(solution)/shard_map/shared_pair/pallas_call | solution.py:236
  115.7 26.9 %all_to_all.16 = bf16[32,48,256]{2,1,0:T(8,128)(2,1)S(1)} all-to-all(bf16[32,48,256]{2,1,0:T(8,128)(2,1)S(1)} %shared_pair.1), channel_id=1, replica_groups=mesh['row'=8,'col'=32] {'col'}, dimensions={0} | all-to-all | bytes 1572864 | tf_op jit(solution)/shard_map/all_to_all | solution.py:321
  142.5 1.2 result.1
  (1 shorter events, 0.0 us)
Async XLA Ops:
  0.0 14.4 %copy-start = (f32[256]{0:T(256)S(1)}, f32[256]{0:T(256)}, u32[]{:S(2)}) copy-start(f32[256]{0:T(256)} %param.12) | copy-start | bytes 3076
  5.1 43.5 %all-to-all-start = ((bf16[8,3,2,8,32,128]{5,4,3,2,1,0:T(8,128)(2,1)}), bf16[8,3,2,8,32,128]{5,4,3,2,1,0:T(8,128)(2,1)}, u32[]{:S(2)}, u32[]{:S(2)}) async-start(bf16[8,3,2,8,32,128]{5,4,3,2,1,0:T(8,128)(2,1)} %flux.1), calls=%async_computation | async-start | bytes 6291456 | tf_op jit(solution)/shard_map/all_to_all | solution.py:289
  48.6 61.4 %copy-start.4 = (bf16[256,256]{1,0:T(8,128)(2,1)S(1)}, bf16[256,256]{1,0:T(8,128)(2,1)}, u32[]{:S(2)}) copy-start(bf16[256,256]{1,0:T(8,128)(2,1)} %get-tuple-element.11.r_ref) | copy-start | bytes 393220
  48.6 61.4 %copy-start.5 = (f32[1024]{0:T(1024)S(1)}, f32[1024]{0:T(1024)}, u32[]{:S(2)}) copy-start(f32[1024]{0:T(1024)} %param.17) | copy-start | bytes 12292
  52.8 57.1 %copy-start.1 = (bf16[1024,1024]{1,0:T(8,128)(2,1)S(1)}, bf16[1024,1024]{1,0:T(8,128)(2,1)}, u32[]{:S(2)}) copy-start(bf16[1024,1024]{1,0:T(8,128)(2,1)} %b_ref.1) | copy-start | bytes 6291460
  52.8 57.1 %copy-start.2 = (bf16[1024,1024]{1,0:T(8,128)(2,1)S(1)}, bf16[1024,1024]{1,0:T(8,128)(2,1)}, u32[]{:S(2)}) copy-start(bf16[1024,1024]{1,0:T(8,128)(2,1)} %a_ref.3) | copy-start | bytes 6291460
  108.4 4.8 %collective-permute-start = (bf16[8,32,8,128]{3,2,1,0:T(8,128)(2,1)S(1)}, bf16[8,32,8,128]{3,2,1,0:T(8,128)(2,1)S(1)}, u32[]{:S(2)}, u32[]{:S(2)}) collective-permute-start(bf16[8,32,8,128]{3,2,1,0:T(8,128)(2,1)S(1)} %slice.4.own_ref), channel_id=1, source_target_pairs={{0,1},{1,0},{2,3},{3,2},{4,5},{5,4},{6,7},{7,6},{8,9},{9,8},{10,11... | collective-permute-start | bytes 1572872 | tf_op jit(solution)/shard_map/ppermute | solution.py:313
  110.0 3.2 %copy-start.3 = (bf16[256,256]{1,0:T(8,128)(2,1)S(1)}, bf16[256,256]{1,0:T(8,128)(2,1)}, u32[]{:S(2)}) copy-start(bf16[256,256]{1,0:T(8,128)(2,1)} %get-tuple-element.13.r_ref) | copy-start | bytes 393220

commit v2 on v0

--- a/solution.py
+++ b/solution.py
@@ -12,7 +12,9 @@
 BF = jnp.bfloat16
 F32 = jnp.float32
 NT_DIMS = (((1,), (1,)), ((), ()))
-VMEM_BYTES = 48 * 1024 * 1024
+MIB = 1024 * 1024
+SPECTRA_LIMIT = 24 * MIB
+SOLVE_LIMIT = 24 * MIB
 
 
 def azimuth_table(mode_count, angle_count, circle):
@@ -38,7 +40,7 @@
         value = value.reshape(z_rows, t_rows, r_rows)
         for group in range(4):
             for half in range(2):
-                x_ref[group * 2 + half, field] = value[
+                x_ref[group * 2 + half, field, 0] = value[
                     group * 8 : group * 8 + 8, :, half * 128 : half * 128 + 128
                 ]
 
@@ -56,7 +58,7 @@
 
 def flux_call(velocity, adj_temp, radial_div):
     _, nt, nz, nr = velocity.shape
-    step = 16
+    step = 32
     return pl.pallas_call(
         flux_kernel,
         grid=(nt // step,),
@@ -65,9 +67,9 @@
             pl.BlockSpec((step, nz, nr), lambda i: (i, 0, 0)),
             pl.BlockSpec((nr, nr), lambda i: (0, 0)),
         ],
-        out_specs=pl.BlockSpec((8, 3, 8, step, 128), lambda i: (0, 0, 0, i, 0)),
-        out_shape=jax.ShapeDtypeStruct((8, 3, 8, nt, 128), BF),
-        compiler_params=pltpu.CompilerParams(vmem_limit_bytes=VMEM_BYTES),
+        out_specs=pl.BlockSpec((8, 3, 1, 8, step, 128), lambda i: (0, 0, i, 0, 0, 0)),
+        out_shape=jax.ShapeDtypeStruct((8, 3, nt // step, 8, step, 128), BF),
+        compiler_params=pltpu.CompilerParams(vmem_limit_bytes=60 * MIB),
         name="flux",
     )(velocity, adj_temp, radial_div)
 
@@ -84,7 +86,9 @@
 
         def transform(field):
             columns = [
-                jnp.concatenate([x_ref[s, field, z + k] for s in range(8)], axis=0)
+                jnp.concatenate(
+                    [x_ref[s, field, h, z + k] for s in range(8) for h in range(2)], axis=0
+                )
                 for k in range(2)
             ]
             return jnp.dot(
@@ -122,7 +126,7 @@
         out_specs=vmem(),
         out_shape=jax.ShapeDtypeStruct((8, 16, 2, 24, 128), BF),
         scratch_shapes=[pltpu.VMEM((table.shape[0] * 16, 128), F32)],
-        compiler_params=pltpu.CompilerParams(vmem_limit_bytes=VMEM_BYTES),
+        compiler_params=pltpu.CompilerParams(vmem_limit_bytes=SPECTRA_LIMIT),
         name="spectra",
     )(fields, table, recip_half)
 
@@ -131,6 +135,7 @@
     nz = hs_ref.shape[0]
     tile = 256
     flux = hf_ref[...].astype(BF)
+    shift = jnp.transpose(jnp.broadcast_to(mu_ref[...], (8, nz)))[:, 0:1] + HEAT_OFFSET
     for at in range(0, nz, tile):
         combined = hs_ref[at : at + tile, :] + jnp.dot(
             a_ref[at : at + tile, :], flux, preferred_element_type=F32
@@ -139,7 +144,7 @@
     combined = low_ref[...]
     for at in range(0, nz, tile):
         coefficient = jnp.dot(bt_ref[at : at + tile, :], combined, preferred_element_type=F32)
-        coefficient = coefficient / (lam_ref[...] + mu_ref[at : at + tile, :] + HEAT_OFFSET)
+        coefficient = coefficient / (lam_ref[...] + shift[at : at + tile, :])
         hf_ref[at : at + tile, :] = coefficient
     coefficients = hf_ref[...].astype(BF)
     out_rows = b_ref.shape[0]
@@ -212,7 +217,7 @@
         out_specs=vmem(),
         out_shape=jax.ShapeDtypeStruct((32, 32, 256), BF),
         scratch_shapes=solve_scratch(),
-        compiler_params=pltpu.CompilerParams(vmem_limit_bytes=VMEM_BYTES),
+        compiler_params=pltpu.CompilerParams(vmem_limit_bytes=SOLVE_LIMIT),
         cost_estimate=pl.CostEstimate(flops=4 * 10**9, bytes_accessed=8 * 10**6, transcendentals=0),
         name="whole_pair",
     )(lines, a, bt, b, r, lam, mu)
@@ -225,7 +230,7 @@
         out_specs=vmem(),
         out_shape=jax.ShapeDtypeStruct((32, 48, 256), BF),
         scratch_shapes=solve_scratch(),
-        compiler_params=pltpu.CompilerParams(vmem_limit_bytes=VMEM_BYTES),
+        compiler_params=pltpu.CompilerParams(vmem_limit_bytes=SOLVE_LIMIT),
         name="shared_pair",
     )(core, own, other, whole, a, bt, b, r, lam, mu)
 
@@ -246,7 +251,7 @@
         in_specs=[vmem()],
         out_specs=vmem(),
         out_shape=jax.ShapeDtypeStruct((mode_rows, 2, 32, 256), F32),
-        compiler_params=pltpu.CompilerParams(vmem_limit_bytes=VMEM_BYTES),
+        compiler_params=pltpu.CompilerParams(vmem_limit_bytes=SOLVE_LIMIT),
         name="result",
     )(pieces)
 
@@ -274,31 +279,35 @@
 
     fields = exchange(flux_call(velocity, adj_temp, radial_div), "row")
 
+    def pick(array, index):
+        return lax.dynamic_index_in_dim(array, index, 0, keepdims=False)
+
     table = azimuth_table(mode_rows * row_total, circle, circle)
     recip_half = lax.dynamic_slice_in_dim(reciprocal_distance, (row_place % 2) * 128, 128)
+    basis_turned = axial_basis.T
+    basis_half = pick(
+        axial_basis.reshape(col_total, 2, 16, axial_basis.shape[1]).swapaxes(0, 1), core
+    ).reshape(col_total * 16, axial_basis.shape[1])
+    shared_mode = 16 + jnp.minimum(chip, 2 * (mode_rows - 16) - 1) // 2
+    mu = axial_eig[None, :]
+    whole_basis, shared_basis = pick(radial_basis, chip), pick(radial_basis, shared_mode)
+    whole_eig, shared_eig = pick(radial_eig, chip)[None, :], pick(radial_eig, shared_mode)[None, :]
+
+    later = [basis_turned, basis_half, whole_basis, shared_basis, whole_eig, shared_eig]
+    fields, later = lax.optimization_barrier((fields, later))
+    basis_turned, basis_half, whole_basis, shared_basis, whole_eig, shared_eig = later
     spectra = spectra_call(fields, table, recip_half[None, :])
     lines = exchange(spectra.reshape(row_total * col_total, 24, 128), ("row", "col"))
     lines = lines.reshape(row_total, col_total, 24, 128)
 
     own = lines[:, :, 16:24, :]
     other = lax.ppermute(own, "col", [(i, i ^ 1) for i in range(col_total)])
-    basis_turned = axial_basis.T
-    basis_half = lax.dynamic_index_in_dim(
-        axial_basis.reshape(col_total, 2, 16, axial_basis.shape[1]), core, 1, keepdims=False
-    ).reshape(col_total * 16, axial_basis.shape[1])
-    shared_mode = 16 + jnp.minimum(chip, 2 * (mode_rows - 16) - 1) // 2
-    mu = axial_eig[:, None]
-
-    def pick(array, index):
-        return lax.dynamic_index_in_dim(array, index, 0, keepdims=False)
-
     whole = whole_call(
-        lines, axial_diff, basis_turned, axial_basis, pick(radial_basis, chip),
-        pick(radial_eig, chip)[None, :], mu,
+        lines, axial_diff, basis_turned, axial_basis, whole_basis, whole_eig, mu
     )
     pieces = shared_call(
         core.reshape(1), own, other, whole, axial_diff, basis_turned, basis_half,
-        pick(radial_basis, shared_mode), pick(radial_eig, shared_mode)[None, :], mu,
+        shared_basis, shared_eig, mu,
     )
     pieces = exchange(pieces, "col")
     return out_call(pieces.reshape(16, 2, 48, 256), mode_rows)

time: 156 us -> 142 us (0.910)
  blocking collectives: 26.9 us -> 82 us
  waiting for transfers between devices: 76.7 us -> 27.1 us
  starting transfers between devices: 21.3 us -> 7.95 us
  Pallas kernels: 18 us -> 13.8 us
  local copies, waits for them, and re-layouts: 11.3 us -> 8.88 us
    all_to_all x0 -> x1, blocking collectives: none -> 55.1 us  [body(): exchange(spectra.reshape(row_total * col_total, 24, 128), ('row', 'col'))]
    all_to_all x1 -> x0, waiting for transfers between devices: 40.9 us -> none  [body(): exchange(spectra.reshape(row_total * col_total, 24, 128), ('row', 'col'))]
    all_to_all x1 -> x0, starting transfers between devices: 13.4 us -> none  [body(): exchange(spectra.reshape(row_total * col_total, 24, 128), ('row', 'col'))]
    all_to_all x1, waiting for transfers between devices: 35.7 us -> 27.1 us  [body(): fields = exchange(flux_call(velocity, adj_temp, radial_div), 'row')]
    unnamed x13 -> x17, local copies, waits for them, and re-layouts: 7.67 us -> 3.97 us
    another operation x0 -> x1, local copies, waits for them, and re-layouts: none -> 2.32 us
    pallas_call x1, Pallas kernels: 5.35 us -> 3.14 us  [whole_call(): pl.pallas_call(whole_kernel, in_specs=[vmem()] * 7, out_specs=vmem(), out...]
    pallas_call x1, Pallas kernels: 4.08 us -> 2.48 us  [shared_call(): pl.pallas_call(shared_kernel, in_specs=[pl.BlockSpec(memory_space=pltpu.S...]
  transfers between devices with their start and end apart: 3 -> 2, of which waited for: 2 -> 1; matrix products, arithmetic and copies ran while one was open for 6% -> 7% of each run, Pallas kernels for 3% -> 2%
where the time goes in v2:
time: 142 us; the launch traced here: 141 us
  blocking collectives  82 us (58%)
  waiting for transfers between devices  27.1 us (19%)
  Pallas kernels  13.8 us (10%)
  local copies, waits for them, and re-layouts  8.88 us (6%)
  starting transfers between devices  7.95 us (6%)
  other arithmetic  1.46 us (1%)
    all_to_all x1, blocking collectives, body(): exchange(spectra.reshape(row_total * col_total, 24, 128), ('row', 'col'))  55.1 us
    all_to_all x1, waiting for transfers between devices, body(): fields = exchange(flux_call(velocity, adj_temp, radial_div), 'row')  27.1 us
    all_to_all x1, blocking collectives, body(): pieces = exchange(pieces, 'col')  26.9 us
    all_to_all x1, starting transfers between devices, body(): fields = exchange(flux_call(velocity, adj_temp, radial_div), 'row')  6.37 us
    pallas_call x1, Pallas kernels, flux_call(): pl.pallas_call(flux_kernel, grid=(nt // step,), in_specs=[pl.BlockSpec((3...  5.06 us
    unnamed x17, local copies, waits for them, and re-layouts  3.97 us
    pallas_call x1, Pallas kernels, whole_call(): pl.pallas_call(whole_kernel, in_specs=[vmem()] * 7, out_specs=vmem(), out...  3.14 us
  transfers between devices with their start and end apart: 2, of which 1 were waited for; matrix products, arithmetic and copies ran while one was open for 7% of the time, Pallas kernels for 2%

profile of v2, /device:TPU:1, one launch (start us, length us, event | category | flops | bytes accessed | tf_op | source)
XLA Modules:
  0.0 141.3 jit_solution(2254616136737571789)
XLA Ops:
  0.0 0.0 copy-start
  0.0 5.1 %flux.1 = bf16[8,3,2,8,32,128]{5,4,3,2,1,0:T(8,128)(2,1)} custom-call(bf16[3,64,32,256]{3,2,1,0:T(8,128)(2,1)} %v_ref.1, bf16[64,32,256]{2,1,0:T(8,128)(2,1)} %t_ref.1, bf16[256,256]{1,0:T(8,128)(2,1)} %d_ref.1), custom_call_target="tpu_custom_call" | custom-call | tf_op jit(solution)/shard_map/flux/pallas_call | solution.py:62
  5.1 6.4 %all-to-all-start = ((bf16[8,3,2,8,32,128]{5,4,3,2,1,0:T(8,128)(2,1)}), bf16[8,3,2,8,32,128]{5,4,3,2,1,0:T(8,128)(2,1)S(1)}, u32[]{:S(2)}, u32[]{:S(2)}) async-start(bf16[8,3,2,8,32,128]{5,4,3,2,1,0:T(8,128)(2,1)} %flux.1), calls=%async_computation | async-start | bytes 6291456 | tf_op jit(solution)/shard_map/all_to_all | solution.py:280
  11.4 3.9 %copy.10 = bf16[1024,1024]{0,1:T(8,128)(2,1)} copy(bf16[1024,1024]{1,0:T(8,128)(2,1)} %b_ref.1) | data formatting | bytes 4194304 | tf_op args[7]
  15.4 0.0 copy-done
  15.4 0.1 dynamic-slice_bitcast_fusion.2.recip_ref
  15.4 0.7 constant_dynamic-slice_fusion
  16.2 1.7 %dynamic-slice_bitcast_fusion = (bf16[256,256]{1,0:T(8,128)(2,1)}, bf16[256,256]{1,0:T(8,128)(2,1)}) fusion(bf16[21,256,256]{2,1,0:T(8,128)(2,1)} %param.13, s32[]{:T(128)S(6)} %select_n.48, s32[]{:T(128)S(6)} %select_n.46), kind=kLoop, calls=%fused_computation.12 | loop fusion | bytes 524296 | tf_op jit(solution)/shard_map/jit(dynamic_index_in_dim)/squeeze | solution.py:283
  17.9 1.4 %multiply_convert_fusion = (bf16[168,512]{1,0:T(8,128)(2,1)S(1)}, bf16[168,512]{1,0:T(8,128)(2,1)S(1)}) fusion(), kind=kLoop, calls=%fused_computation.7 | loop fusion | flops 1634304 | bytes 344064 | tf_op jit(solution)/shard_map/convert.1
  19.3 2.3 %constant_dynamic-slice_fusion.2 = bf16[32,1,16,1024]{3,2,1,0:T(8,128)(2,1)} fusion(bf16[32,2,16,1024]{3,2,1,0:T(8,128)(2,1)} %bitcast.19, s32[]{:T(128)S(6)} %select_n.44), kind=kLoop, calls=%fused_computation.16 | loop fusion | bytes 2097156 | tf_op jit(solution)/shard_map/dynamic-slice
  21.7 27.1 %all-to-all-done.x_ref = bf16[8,3,2,8,32,128]{5,4,3,2,1,0:T(8,128)(2,1)S(1)} async-done(((bf16[8,3,2,8,32,128]{5,4,3,2,1,0:T(8,128)(2,1)}), bf16[8,3,2,8,32,128]{5,4,3,2,1,0:T(8,128)(2,1)S(1)}, u32[]{:S(2)}, u32[]{:S(2)}) %all-to-all-start) | async-done | bytes 3145760 | tf_op jit(solution)/shard_map/all_to_all | solution.py:280
  48.7 0.0 copy-start.4
  48.7 2.0 %spectra.1 = bf16[8,16,2,24,128]{4,3,2,1,0:T(8,128)(2,1)S(1)} custom-call(bf16[8,3,2,8,32,128]{5,4,3,2,1,0:T(8,128)(2,1)S(1)} %all-to-all-done.x_ref, bf16[336,512]{1,0:T(8,128)(2,1)S(1)} %pad_maximum_fusion.w_ref, f32[1,128]{1,0:T(1,128)S(1)} %dynamic-slice_bitcast_fusion.2.recip_ref), custom_call_target="tpu_custom_call" | custom-call | tf_op jit(solution)/shard_map/spectra/pallas_call | solution.py:123
  50.7 0.0 copy-start.1
  50.7 0.0 copy-start.2
  50.7 55.1 %all_to_all.15 = bf16[256,24,128]{2,1,0:T(8,128)(2,1)S(1)} all-to-all(bf16[256,24,128]{2,1,0:T(8,128)(2,1)S(1)} %bitcast.18), channel_id=1, replica_groups=mesh['row'=8,'col'=32] {'row','col'}, dimensions={0} | all-to-all | bytes 3145728 | tf_op jit(solution)/shard_map/all_to_all | solution.py:300
  105.9 0.1 slice.4.own_ref
  106.0 1.6 %collective-permute-start = (bf16[8,32,8,128]{3,2,1,0:T(8,128)(2,1)S(1)}, bf16[8,32,8,128]{3,2,1,0:T(8,128)(2,1)S(1)}, u32[]{:S(2)}, u32[]{:S(2)}) collective-permute-start(bf16[8,32,8,128]{3,2,1,0:T(8,128)(2,1)S(1)} %slice.4.own_ref), channel_id=1, source_target_pairs={{0,1},{1,0},{2,3},{3,2},{4,5},{5,4},{6,7},{7,6},{8,9},{9,8},{10,11... | collective-permute-start | bytes 1572872 | tf_op jit(solution)/shard_map/ppermute | solution.py:304
  107.5 0.0 copy-done.4
  107.5 0.0 copy-done.6
  107.5 0.0 copy-done.7
  107.5 0.0 copy-done.1
  107.6 0.0 copy-done.2
  107.6 0.0 copy-start.3
  107.6 0.0 copy-start.5
  107.6 3.1 %whole_pair.1.whole_ref = bf16[32,32,256]{2,1,0:T(8,128)(2,1)S(1)} custom-call(bf16[8,32,24,128]{3,2,1,0:T(8,128)(2,1)S(1)} %bitcast.23, bf16[1024,1024]{1,0:T(8,128)(2,1)S(1)} %copy-done.4, bf16[1024,1024]{1,0:T(8,128)(2,1)S(1)} %bitcast.16, bf16[1024,1024]{1,0:T(8,128)(2,1)S(1)} %copy-done.2, bf16[256,256]{1,0:T(8,128)(2,1)S(1)} %copy-done.6, ...), custom_call_target="tpu_custom_call" | custom-call | flops 4000000000 | bytes 8000000 | tf_op jit(solution)/shard_map/whole_pair/pallas_call | solution.py:214
  110.7 0.0 collective-permute-done.other_ref
  110.7 0.0 copy-done.3
  110.8 0.0 copy-done.5
  110.8 2.5 %shared_pair.1 = bf16[32,48,256]{2,1,0:T(8,128)(2,1)S(1)} custom-call(s32[1]{0:T(128)} %bitcast.core_ref, bf16[8,32,8,128]{3,2,1,0:T(8,128)(2,1)S(1)} %slice.4.own_ref, bf16[8,32,8,128]{3,2,1,0:T(8,128)(2,1)S(1)} %collective-permute-done.other_ref, bf16[32,32,256]{2,1,0:T(8,128)(2,1)S(1)} %whole_pair.1.whole_ref, bf16[1024,1024]{1,0:T(8,128)(2,1)S(1)} %copy-done.4, ...), custom_call_target="tpu_custom_call" | custom-call | tf_op jit(solution)/shard_map/shared_pair/pallas_call | solution.py:227
  113.2 26.9 %all_to_all.16 = bf16[32,48,256]{2,1,0:T(8,128)(2,1)S(1)} all-to-all(bf16[32,48,256]{2,1,0:T(8,128)(2,1)S(1)} %shared_pair.1), channel_id=1, replica_groups=mesh['row'=8,'col'=32] {'col'}, dimensions={0} | all-to-all | bytes 1572864 | tf_op jit(solution)/shard_map/all_to_all | solution.py:312
  140.1 1.2 result.1
  (3 shorter events, 0.0 us)
Async XLA Ops:
  0.0 15.4 %copy-start = (f32[256]{0:T(256)S(1)}, f32[256]{0:T(256)}, u32[]{:S(2)}) copy-start(f32[256]{0:T(256)} %param.12) | copy-start | bytes 3076
  5.1 43.7 %all-to-all-start = ((bf16[8,3,2,8,32,128]{5,4,3,2,1,0:T(8,128)(2,1)}), bf16[8,3,2,8,32,128]{5,4,3,2,1,0:T(8,128)(2,1)S(1)}, u32[]{:S(2)}, u32[]{:S(2)}) async-start(bf16[8,3,2,8,32,128]{5,4,3,2,1,0:T(8,128)(2,1)} %flux.1), calls=%async_computation | async-start | bytes 6291456 | tf_op jit(solution)/shard_map/all_to_all | solution.py:280
  48.7 58.8 %copy-start.4 = (bf16[1024,1024]{1,0:T(8,128)(2,1)S(1)}, bf16[1024,1024]{1,0:T(8,128)(2,1)}, u32[]{:S(2)}) copy-start(bf16[1024,1024]{1,0:T(8,128)(2,1)} %a_ref.3) | copy-start | bytes 6291460
  48.7 58.8 %copy-start.6 = (bf16[256,256]{1,0:T(8,128)(2,1)S(1)}, bf16[256,256]{1,0:T(8,128)(2,1)}, u32[]{:S(2)}) copy-start(bf16[256,256]{1,0:T(8,128)(2,1)} %get-tuple-element.14.r_ref) | copy-start | bytes 393220
  48.7 58.8 %copy-start.7 = (f32[1024]{0:T(1024)S(1)}, f32[1024]{0:T(1024)}, u32[]{:S(2)}) copy-start(f32[1024]{0:T(1024)} %param.17) | copy-start | bytes 12292
  50.7 56.9 %copy-start.1 = (bf16[1024,1024]{0,1:T(8,128)(2,1)S(1)}, bf16[1024,1024]{0,1:T(8,128)(2,1)}, u32[]{:S(2)}) copy-start(bf16[1024,1024]{0,1:T(8,128)(2,1)} %copy.10) | copy-start | bytes 6291460
  50.7 56.8 %copy-start.2 = (bf16[1024,1024]{1,0:T(8,128)(2,1)S(1)}, bf16[1024,1024]{1,0:T(8,128)(2,1)}, u32[]{:S(2)}) copy-start(bf16[1024,1024]{1,0:T(8,128)(2,1)} %b_ref.1) | copy-start | bytes 6291460
  106.0 4.8 %collective-permute-start = (bf16[8,32,8,128]{3,2,1,0:T(8,128)(2,1)S(1)}, bf16[8,32,8,128]{3,2,1,0:T(8,128)(2,1)S(1)}, u32[]{:S(2)}, u32[]{:S(2)}) collective-permute-start(bf16[8,32,8,128]{3,2,1,0:T(8,128)(2,1)S(1)} %slice.4.own_ref), channel_id=1, source_target_pairs={{0,1},{1,0},{2,3},{3,2},{4,5},{5,4},{6,7},{7,6},{8,9},{9,8},{10,11... | collective-permute-start | bytes 1572872 | tf_op jit(solution)/shard_map/ppermute | solution.py:304
  107.6 3.2 %copy-start.3 = (bf16[32,1,16,1024]{3,2,1,0:T(8,128)(2,1)S(1)}, bf16[32,1,16,1024]{3,2,1,0:T(8,128)(2,1)}, u32[]{:S(2)}) copy-start(bf16[32,1,16,1024]{3,2,1,0:T(8,128)(2,1)} %constant_dynamic-slice_fusion.2) | copy-start | bytes 3145732
  107.6 3.2 %copy-start.5 = (bf16[256,256]{1,0:T(8,128)(2,1)S(1)}, bf16[256,256]{1,0:T(8,128)(2,1)}, u32[]{:S(2)}) copy-start(bf16[256,256]{1,0:T(8,128)(2,1)} %get-tuple-element.17.r_ref) | copy-start | bytes 393220

commit v3 on v2

--- a/solution.py
+++ b/solution.py
@@ -37,23 +37,18 @@
     temp = t_ref[...].astype(F32)
 
     def put(field, value):
-        value = value.reshape(z_rows, t_rows, r_rows)
+        value = jnp.swapaxes(value, 0, 1).astype(BF)
         for group in range(4):
             for half in range(2):
                 x_ref[group * 2 + half, field, 0] = value[
                     group * 8 : group * 8 + 8, :, half * 128 : half * 128 + 128
                 ]
 
-    def flux(c):
-        product = v_ref[c].astype(F32) * temp
-        return jnp.swapaxes(product, 0, 1).astype(BF)
-
-    put(1, flux(1))
-    put(2, flux(2))
-    radial = flux(0).reshape(z_rows * t_rows, r_rows)
-    turned_temp = jnp.swapaxes(temp, 0, 1).reshape(z_rows * t_rows, r_rows)
+    put(1, v_ref[1].astype(F32) * temp)
+    put(2, v_ref[2].astype(F32) * temp)
+    radial = (v_ref[0].astype(F32) * temp).astype(BF).reshape(t_rows * z_rows, r_rows)
     div = lax.dot_general(radial, d_ref[...], NT_DIMS, preferred_element_type=F32)
-    put(0, (HEAT_OFFSET * turned_temp + div).astype(BF))
+    put(0, HEAT_OFFSET * temp + div.reshape(t_rows, z_rows, r_rows))
 
 
 def flux_call(velocity, adj_temp, radial_div):
@@ -125,7 +120,7 @@
         in_specs=[vmem()] * 3,
         out_specs=vmem(),
         out_shape=jax.ShapeDtypeStruct((8, 16, 2, 24, 128), BF),
-        scratch_shapes=[pltpu.VMEM((table.shape[0] * 16, 128), F32)],
+        scratch_shapes=[pltpu.VMEM((table.shape[0] * 16 + 16, 128), F32)],
         compiler_params=pltpu.CompilerParams(vmem_limit_bytes=SPECTRA_LIMIT),
         name="spectra",
     )(fields, table, recip_half)
@@ -133,7 +128,7 @@
 
 def axial_solve(hs_ref, hf_ref, low_ref, a_ref, bt_ref, b_ref, r_ref, lam_ref, mu_ref, put):
     nz = hs_ref.shape[0]
-    tile = 256
+    tile = 512
     flux = hf_ref[...].astype(BF)
     shift = jnp.transpose(jnp.broadcast_to(mu_ref[...], (8, nz)))[:, 0:1] + HEAT_OFFSET
     for at in range(0, nz, tile):
@@ -142,11 +137,12 @@
         )
         low_ref[at : at + tile, :] = combined.astype(BF)
     combined = low_ref[...]
+    coefficients = []
     for at in range(0, nz, tile):
         coefficient = jnp.dot(bt_ref[at : at + tile, :], combined, preferred_element_type=F32)
         coefficient = coefficient / (lam_ref[...] + shift[at : at + tile, :])
-        hf_ref[at : at + tile, :] = coefficient
-    coefficients = hf_ref[...].astype(BF)
+        coefficients.append(coefficient.astype(BF))
+    coefficients = jnp.concatenate(coefficients, axis=0)
     out_rows = b_ref.shape[0]
     for at in range(0, out_rows, tile):
         returned = jnp.dot(b_ref[at : at + tile, :], coefficients, preferred_element_type=F32)

time: 142 us -> 141 us (level)
  no operation moved by 1% of the time
where the time goes in v3:
time: 141 us
  blocking collectives  82 us (58%)
  waiting for transfers between devices  27.1 us (19%)
  Pallas kernels  13.2 us (9%)
  local copies, waits for them, and re-layouts  8.88 us (6%)
  starting transfers between devices  7.95 us (6%)
  other arithmetic  1.46 us (1%)
    all_to_all x1, blocking collectives, body(): exchange(spectra.reshape(row_total * col_total, 24, 128), ('row', 'col'))  55.1 us
    all_to_all x1, waiting for transfers between devices, body(): fields = exchange(flux_call(velocity, adj_temp, radial_div), 'row')  27.1 us
    all_to_all x1, blocking collectives, body(): pieces = exchange(pieces, 'col')  26.9 us
    all_to_all x1, starting transfers between devices, body(): fields = exchange(flux_call(velocity, adj_temp, radial_div), 'row')  6.37 us
    pallas_call x1, Pallas kernels, flux_call(): pl.pallas_call(flux_kernel, grid=(nt // step,), in_specs=[pl.BlockSpec((3...  4.65 us
    unnamed x17, local copies, waits for them, and re-layouts  3.97 us
    pallas_call x1, Pallas kernels, whole_call(): pl.pallas_call(whole_kernel, in_specs=[vmem()] * 7, out_specs=vmem(), out...  3 us
  transfers between devices with their start and end apart: 2, of which 1 were waited for; matrix products, arithmetic and copies ran while one was open for 7% of the time, Pallas kernels for 2%

profile of v3, /device:TPU:1, one launch (start us, length us, event | category | flops | bytes accessed | tf_op | source)
XLA Modules:
  0.0 140.7 jit_solution(16504361355368933256)
XLA Ops:
  0.0 0.0 copy-start
  0.0 4.7 %flux.1 = bf16[8,3,2,8,32,128]{5,4,3,2,1,0:T(8,128)(2,1)} custom-call(bf16[3,64,32,256]{3,2,1,0:T(8,128)(2,1)} %v_ref.1, bf16[64,32,256]{2,1,0:T(8,128)(2,1)} %t_ref.1, bf16[256,256]{1,0:T(8,128)(2,1)} %d_ref.1), custom_call_target="tpu_custom_call" | custom-call | tf_op jit(solution)/shard_map/flux/pallas_call | solution.py:57
  4.7 6.4 %all-to-all-start = ((bf16[8,3,2,8,32,128]{5,4,3,2,1,0:T(8,128)(2,1)}), bf16[8,3,2,8,32,128]{5,4,3,2,1,0:T(8,128)(2,1)S(1)}, u32[]{:S(2)}, u32[]{:S(2)}) async-start(bf16[8,3,2,8,32,128]{5,4,3,2,1,0:T(8,128)(2,1)} %flux.1), calls=%async_computation | async-start | bytes 6291456 | tf_op jit(solution)/shard_map/all_to_all | solution.py:276
  11.0 3.9 %copy.10 = bf16[1024,1024]{0,1:T(8,128)(2,1)} copy(bf16[1024,1024]{1,0:T(8,128)(2,1)} %b_ref.1) | data formatting | bytes 4194304 | tf_op args[7]
  15.0 0.0 copy-done
  15.0 0.1 dynamic-slice_bitcast_fusion.2.recip_ref
  15.0 0.7 constant_dynamic-slice_fusion
  15.8 1.7 %dynamic-slice_bitcast_fusion = (bf16[256,256]{1,0:T(8,128)(2,1)}, bf16[256,256]{1,0:T(8,128)(2,1)}) fusion(bf16[21,256,256]{2,1,0:T(8,128)(2,1)} %param.13, s32[]{:T(128)S(6)} %select_n.48, s32[]{:T(128)S(6)} %select_n.46), kind=kLoop, calls=%fused_computation.12 | loop fusion | bytes 524296 | tf_op jit(solution)/shard_map/jit(dynamic_index_in_dim)/squeeze | solution.py:279
  17.5 1.4 %multiply_convert_fusion = (bf16[168,512]{1,0:T(8,128)(2,1)S(1)}, bf16[168,512]{1,0:T(8,128)(2,1)S(1)}) fusion(), kind=kLoop, calls=%fused_computation.7 | loop fusion | flops 1634304 | bytes 344064 | tf_op jit(solution)/shard_map/convert.1
  18.9 2.3 %constant_dynamic-slice_fusion.2 = bf16[32,1,16,1024]{3,2,1,0:T(8,128)(2,1)} fusion(bf16[32,2,16,1024]{3,2,1,0:T(8,128)(2,1)} %bitcast.19, s32[]{:T(128)S(6)} %select_n.44), kind=kLoop, calls=%fused_computation.16 | loop fusion | bytes 2097156 | tf_op jit(solution)/shard_map/dynamic-slice
  21.3 27.1 %all-to-all-done.x_ref = bf16[8,3,2,8,32,128]{5,4,3,2,1,0:T(8,128)(2,1)S(1)} async-done(((bf16[8,3,2,8,32,128]{5,4,3,2,1,0:T(8,128)(2,1)}), bf16[8,3,2,8,32,128]{5,4,3,2,1,0:T(8,128)(2,1)S(1)}, u32[]{:S(2)}, u32[]{:S(2)}) %all-to-all-start) | async-done | bytes 3145760 | tf_op jit(solution)/shard_map/all_to_all | solution.py:276
  48.3 0.0 copy-start.4
  48.3 2.0 %spectra.1 = bf16[8,16,2,24,128]{4,3,2,1,0:T(8,128)(2,1)S(1)} custom-call(bf16[8,3,2,8,32,128]{5,4,3,2,1,0:T(8,128)(2,1)S(1)} %all-to-all-done.x_ref, bf16[336,512]{1,0:T(8,128)(2,1)S(1)} %pad_maximum_fusion.w_ref, f32[1,128]{1,0:T(1,128)S(1)} %dynamic-slice_bitcast_fusion.2.recip_ref), custom_call_target="tpu_custom_call" | custom-call | tf_op jit(solution)/shard_map/spectra/pallas_call | solution.py:118
  50.3 0.0 copy-start.1
  50.3 0.0 copy-start.2
  50.3 55.1 %all_to_all.15 = bf16[256,24,128]{2,1,0:T(8,128)(2,1)S(1)} all-to-all(bf16[256,24,128]{2,1,0:T(8,128)(2,1)S(1)} %bitcast.18), channel_id=1, replica_groups=mesh['row'=8,'col'=32] {'row','col'}, dimensions={0} | all-to-all | bytes 3145728 | tf_op jit(solution)/shard_map/all_to_all | solution.py:296
  105.5 0.1 slice.4.own_ref
  105.6 1.6 %collective-permute-start = (bf16[8,32,8,128]{3,2,1,0:T(8,128)(2,1)S(1)}, bf16[8,32,8,128]{3,2,1,0:T(8,128)(2,1)S(1)}, u32[]{:S(2)}, u32[]{:S(2)}) collective-permute-start(bf16[8,32,8,128]{3,2,1,0:T(8,128)(2,1)S(1)} %slice.4.own_ref), channel_id=1, source_target_pairs={{0,1},{1,0},{2,3},{3,2},{4,5},{5,4},{6,7},{7,6},{8,9},{9,8},{10,11... | collective-permute-start | bytes 1572872 | tf_op jit(solution)/shard_map/ppermute | solution.py:300
  107.2 0.0 copy-done.4
  107.2 0.0 copy-done.6
  107.2 0.0 copy-done.7
  107.2 0.0 copy-done.1
  107.2 0.0 copy-done.2
  107.2 0.0 copy-start.3
  107.2 0.0 copy-start.5
  107.2 3.0 %whole_pair.1.whole_ref = bf16[32,32,256]{2,1,0:T(8,128)(2,1)S(1)} custom-call(bf16[8,32,24,128]{3,2,1,0:T(8,128)(2,1)S(1)} %bitcast.23, bf16[1024,1024]{1,0:T(8,128)(2,1)S(1)} %copy-done.4, bf16[1024,1024]{1,0:T(8,128)(2,1)S(1)} %bitcast.16, bf16[1024,1024]{1,0:T(8,128)(2,1)S(1)} %copy-done.2, bf16[256,256]{1,0:T(8,128)(2,1)S(1)} %copy-done.6, ...), custom_call_target="tpu_custom_call" | custom-call | flops 4000000000 | bytes 8000000 | tf_op jit(solution)/shard_map/whole_pair/pallas_call | solution.py:210
  110.2 0.0 collective-permute-done.other_ref
  110.2 0.0 copy-done.3
  110.2 0.0 copy-done.5
  110.2 2.4 %shared_pair.1 = bf16[32,48,256]{2,1,0:T(8,128)(2,1)S(1)} custom-call(s32[1]{0:T(128)} %bitcast.core_ref, bf16[8,32,8,128]{3,2,1,0:T(8,128)(2,1)S(1)} %slice.4.own_ref, bf16[8,32,8,128]{3,2,1,0:T(8,128)(2,1)S(1)} %collective-permute-done.other_ref, bf16[32,32,256]{2,1,0:T(8,128)(2,1)S(1)} %whole_pair.1.whole_ref, bf16[1024,1024]{1,0:T(8,128)(2,1)S(1)} %copy-done.4, ...), custom_call_target="tpu_custom_call" | custom-call | tf_op jit(solution)/shard_map/shared_pair/pallas_call | solution.py:223
  112.7 26.9 %all_to_all.16 = bf16[32,48,256]{2,1,0:T(8,128)(2,1)S(1)} all-to-all(bf16[32,48,256]{2,1,0:T(8,128)(2,1)S(1)} %shared_pair.1), channel_id=1, replica_groups=mesh['row'=8,'col'=32] {'col'}, dimensions={0} | all-to-all | bytes 1572864 | tf_op jit(solution)/shard_map/all_to_all | solution.py:308
  139.5 1.2 result.1
  (3 shorter events, 0.0 us)
Async XLA Ops:
  0.0 15.0 %copy-start = (f32[256]{0:T(256)S(1)}, f32[256]{0:T(256)}, u32[]{:S(2)}) copy-start(f32[256]{0:T(256)} %param.12) | copy-start | bytes 3076
  4.7 43.7 %all-to-all-start = ((bf16[8,3,2,8,32,128]{5,4,3,2,1,0:T(8,128)(2,1)}), bf16[8,3,2,8,32,128]{5,4,3,2,1,0:T(8,128)(2,1)S(1)}, u32[]{:S(2)}, u32[]{:S(2)}) async-start(bf16[8,3,2,8,32,128]{5,4,3,2,1,0:T(8,128)(2,1)} %flux.1), calls=%async_computation | async-start | bytes 6291456 | tf_op jit(solution)/shard_map/all_to_all | solution.py:276
  48.3 58.8 %copy-start.4 = (bf16[1024,1024]{1,0:T(8,128)(2,1)S(1)}, bf16[1024,1024]{1,0:T(8,128)(2,1)}, u32[]{:S(2)}) copy-start(bf16[1024,1024]{1,0:T(8,128)(2,1)} %a_ref.3) | copy-start | bytes 6291460
  48.3 58.8 %copy-start.6 = (bf16[256,256]{1,0:T(8,128)(2,1)S(1)}, bf16[256,256]{1,0:T(8,128)(2,1)}, u32[]{:S(2)}) copy-start(bf16[256,256]{1,0:T(8,128)(2,1)} %get-tuple-element.14.r_ref) | copy-start | bytes 393220
  48.3 58.8 %copy-start.7 = (f32[1024]{0:T(1024)S(1)}, f32[1024]{0:T(1024)}, u32[]{:S(2)}) copy-start(f32[1024]{0:T(1024)} %param.17) | copy-start | bytes 12292
  50.3 56.8 %copy-start.1 = (bf16[1024,1024]{0,1:T(8,128)(2,1)S(1)}, bf16[1024,1024]{0,1:T(8,128)(2,1)}, u32[]{:S(2)}) copy-start(bf16[1024,1024]{0,1:T(8,128)(2,1)} %copy.10) | copy-start | bytes 6291460
  50.3 56.8 %copy-start.2 = (bf16[1024,1024]{1,0:T(8,128)(2,1)S(1)}, bf16[1024,1024]{1,0:T(8,128)(2,1)}, u32[]{:S(2)}) copy-start(bf16[1024,1024]{1,0:T(8,128)(2,1)} %b_ref.1) | copy-start | bytes 6291460
  105.6 4.6 %collective-permute-start = (bf16[8,32,8,128]{3,2,1,0:T(8,128)(2,1)S(1)}, bf16[8,32,8,128]{3,2,1,0:T(8,128)(2,1)S(1)}, u32[]{:S(2)}, u32[]{:S(2)}) collective-permute-start(bf16[8,32,8,128]{3,2,1,0:T(8,128)(2,1)S(1)} %slice.4.own_ref), channel_id=1, source_target_pairs={{0,1},{1,0},{2,3},{3,2},{4,5},{5,4},{6,7},{7,6},{8,9},{9,8},{10,11... | collective-permute-start | bytes 1572872 | tf_op jit(solution)/shard_map/ppermute | solution.py:300
  107.2 3.0 %copy-start.3 = (bf16[32,1,16,1024]{3,2,1,0:T(8,128)(2,1)S(1)}, bf16[32,1,16,1024]{3,2,1,0:T(8,128)(2,1)}, u32[]{:S(2)}) copy-start(bf16[32,1,16,1024]{3,2,1,0:T(8,128)(2,1)} %constant_dynamic-slice_fusion.2) | copy-start | bytes 3145732
  107.2 3.0 %copy-start.5 = (bf16[256,256]{1,0:T(8,128)(2,1)S(1)}, bf16[256,256]{1,0:T(8,128)(2,1)}, u32[]{:S(2)}) copy-start(bf16[256,256]{1,0:T(8,128)(2,1)} %get-tuple-element.17.r_ref) | copy-start | bytes 393220

commit v4 on v3

--- a/solution.py
+++ b/solution.py
@@ -3,6 +3,8 @@
 
 import jax
 import jax.numpy as jnp
+import ml_dtypes
+import numpy as np
 from jax import lax
 from jax.experimental import pallas as pl
 from jax.experimental.pallas import tpu as pltpu
@@ -14,27 +16,44 @@
 NT_DIMS = (((1,), (1,)), ((), ()))
 MIB = 1024 * 1024
 SPECTRA_LIMIT = 24 * MIB
+FLUX_LIMIT = 60 * MIB
 SOLVE_LIMIT = 24 * MIB
 
 
 def azimuth_table(mode_count, angle_count, circle):
-    mode_ids = jnp.arange(mode_count, dtype=jnp.int32)
-    angle_ids = jnp.arange(angle_count, dtype=jnp.int32)
+    mode_ids = np.arange(mode_count, dtype=np.int32)
+    angle_ids = np.arange(angle_count, dtype=np.int32)
     phase_index = mode_ids[:, None] * angle_ids[None, :] % circle
-    angle_value = phase_index.astype(F32) * (2.0 * math.pi / circle)
-    norm_factor = 1.0 / math.sqrt(circle)
-    return jnp.concatenate(
-        [jnp.cos(angle_value) * norm_factor, -jnp.sin(angle_value) * norm_factor], axis=0
-    ).astype(BF)
+    angle_value = phase_index.astype(np.float32) * np.float32(2.0 * math.pi / circle)
+    norm_factor = np.float32(1.0 / math.sqrt(circle))
+    return np.concatenate(
+        [np.cos(angle_value) * norm_factor, -np.sin(angle_value) * norm_factor], axis=0
+    ).astype(ml_dtypes.bfloat16)
+
+
+def smem():
+    return pl.BlockSpec(memory_space=pltpu.SMEM)
 
 
 def vmem():
     return pl.BlockSpec(memory_space=pltpu.VMEM)
 
 
-def flux_kernel(v_ref, t_ref, d_ref, x_ref):
+def flux_kernel(
+    chip_ref, extra_ref, v_ref, t_ref, d_ref, basis_ref, x_ref, whole_ref, shared_ref, sems
+):
     t_rows, z_rows, r_rows = t_ref.shape
     temp = t_ref[...].astype(F32)
+    part = pl.program_id(0)
+    picks = [
+        pltpu.make_async_copy(basis_ref.at[index[0]], to, sems.at[k])
+        for k, (index, to) in enumerate(((chip_ref, whole_ref), (extra_ref, shared_ref)))
+    ]
+
+    @pl.when(part == 0)
+    def _():
+        for pick in picks:
+            pick.start()
 
     def put(field, value):
         value = jnp.swapaxes(value, 0, 1).astype(BF)
@@ -50,31 +69,46 @@
     div = lax.dot_general(radial, d_ref[...], NT_DIMS, preferred_element_type=F32)
     put(0, HEAT_OFFSET * temp + div.reshape(t_rows, z_rows, r_rows))
 
-
-def flux_call(velocity, adj_temp, radial_div):
+    @pl.when(part == pl.num_programs(0) - 1)
+    def _():
+        for pick in picks:
+            pick.wait()
+
+
+def flux_call(chip, extra, velocity, adj_temp, radial_div, basis):
     _, nt, nz, nr = velocity.shape
     step = 32
+    anywhere = pl.BlockSpec(memory_space=pl.ANY)
+    matrix = jax.ShapeDtypeStruct(basis.shape[1:], BF)
     return pl.pallas_call(
         flux_kernel,
         grid=(nt // step,),
         in_specs=[
+            smem(),
+            smem(),
             pl.BlockSpec((3, step, nz, nr), lambda i: (0, i, 0, 0)),
             pl.BlockSpec((step, nz, nr), lambda i: (i, 0, 0)),
             pl.BlockSpec((nr, nr), lambda i: (0, 0)),
+            anywhere,
         ],
-        out_specs=pl.BlockSpec((8, 3, 1, 8, step, 128), lambda i: (0, 0, i, 0, 0, 0)),
-        out_shape=jax.ShapeDtypeStruct((8, 3, nt // step, 8, step, 128), BF),
-        compiler_params=pltpu.CompilerParams(vmem_limit_bytes=60 * MIB),
+        out_specs=[
+            pl.BlockSpec((8, 3, 1, 8, step, 128), lambda i: (0, 0, i, 0, 0, 0)),
+            anywhere,
+            anywhere,
+        ],
+        out_shape=[jax.ShapeDtypeStruct((8, 3, nt // step, 8, step, 128), BF), matrix, matrix],
+        scratch_shapes=[pltpu.SemaphoreType.DMA((2,))],
+        compiler_params=pltpu.CompilerParams(vmem_limit_bytes=FLUX_LIMIT),
         name="flux",
-    )(velocity, adj_temp, radial_div)
-
-
-def spectra_kernel(x_ref, w_ref, recip_ref, y_ref, u_ref):
+    )(chip, extra, velocity, adj_temp, radial_div, basis)
+
+
+def spectra_kernel(half_ref, x_ref, w_ref, recip_ref, y_ref, u_ref):
     rows = w_ref.shape[0]
     modes = rows // 2
     table = w_ref[...]
     mode_id = lax.broadcasted_iota(jnp.int32, (modes, 128), 0).astype(F32)
-    scale = mode_id * recip_ref[...]
+    scale = mode_id * jnp.where(half_ref[0] == 0, recip_ref[:, :128], recip_ref[:, 128:])
     scale = jnp.concatenate([scale, scale], axis=0)
     scale = jnp.concatenate([scale, scale], axis=1)
     for z in range(0, 8, 2):
@@ -114,45 +148,50 @@
             y_ref[row, chip, :, 16:24, :] = jnp.zeros((2, 8, 128), BF)
 
 
-def spectra_call(fields, table, recip_half):
+def spectra_call(half, fields, table, recip):
     return pl.pallas_call(
         spectra_kernel,
-        in_specs=[vmem()] * 3,
+        in_specs=[smem()] + [vmem()] * 3,
         out_specs=vmem(),
         out_shape=jax.ShapeDtypeStruct((8, 16, 2, 24, 128), BF),
         scratch_shapes=[pltpu.VMEM((table.shape[0] * 16 + 16, 128), F32)],
         compiler_params=pltpu.CompilerParams(vmem_limit_bytes=SPECTRA_LIMIT),
         name="spectra",
-    )(fields, table, recip_half)
-
-
-def axial_solve(hs_ref, hf_ref, low_ref, a_ref, bt_ref, b_ref, r_ref, lam_ref, mu_ref, put):
+    )(half, fields, table, recip)
+
+
+def axial_solve(hs_ref, hf_ref, low_ref, a_ref, b_ref, out_basis, r_ref, eig_ref, index, mu_ref, put, out_rows):
     nz = hs_ref.shape[0]
+    lines = hs_ref.shape[1]
     tile = 512
     flux = hf_ref[...].astype(BF)
-    shift = jnp.transpose(jnp.broadcast_to(mu_ref[...], (8, nz)))[:, 0:1] + HEAT_OFFSET
+    eig = jnp.broadcast_to(eig_ref[pl.ds(index, 1), :], (8, lines))
+    shift = jnp.transpose(eig)[:, 0:1] + HEAT_OFFSET
     for at in range(0, nz, tile):
         combined = hs_ref[at : at + tile, :] + jnp.dot(
             a_ref[at : at + tile, :], flux, preferred_element_type=F32
         )
         low_ref[at : at + tile, :] = combined.astype(BF)
-    combined = low_ref[...]
+    turned = jnp.transpose(low_ref[...])
     coefficients = []
     for at in range(0, nz, tile):
-        coefficient = jnp.dot(bt_ref[at : at + tile, :], combined, preferred_element_type=F32)
-        coefficient = coefficient / (lam_ref[...] + shift[at : at + tile, :])
+        coefficient = jnp.dot(turned, b_ref[:, at : at + tile], preferred_element_type=F32)
+        coefficient = coefficient / (shift + mu_ref[:, at : at + tile])
         coefficients.append(coefficient.astype(BF))
-    coefficients = jnp.concatenate(coefficients, axis=0)
-    out_rows = b_ref.shape[0]
+    coefficients = jnp.concatenate(coefficients, axis=1)
     for at in range(0, out_rows, tile):
-        returned = jnp.dot(b_ref[at : at + tile, :], coefficients, preferred_element_type=F32)
+        returned = lax.dot_general(
+            out_basis(at, tile), coefficients, NT_DIMS, preferred_element_type=F32
+        )
         value = lax.dot_general(
             returned.astype(BF), r_ref[...], NT_DIMS, preferred_element_type=F32
         )
         put(at, tile, value.astype(BF))
 
 
-def whole_kernel(y_ref, a_ref, bt_ref, b_ref, r_ref, lam_ref, mu_ref, o_ref, hs_ref, hf_ref, low_ref):
+def whole_kernel(
+    chip_ref, y_ref, a_ref, b_ref, r_ref, eig_ref, mu_ref, o_ref, hs_ref, hf_ref, low_ref
+):
     hs4 = hs_ref.reshape(32, 4, 8, 256)
     hf4 = hf_ref.reshape(32, 4, 8, 256)
     for group in range(4):
@@ -166,11 +205,14 @@
     def put(at, tile, value):
         o_ref[at // 32 : (at + tile) // 32] = value.reshape(tile // 32, 32, 256)
 
-    axial_solve(hs_ref, hf_ref, low_ref, a_ref, bt_ref, b_ref, r_ref, lam_ref, mu_ref, put)
+    axial_solve(
+        hs_ref, hf_ref, low_ref, a_ref, b_ref, lambda at, tile: b_ref[at : at + tile, :],
+        r_ref, eig_ref, chip_ref[0], mu_ref, put, 1024,
+    )
 
 
 def shared_kernel(
-    core_ref, own_ref, other_ref, whole_ref, a_ref, bt_ref, b_ref, r_ref, lam_ref, mu_ref,
+    core_ref, extra_ref, own_ref, other_ref, whole_ref, a_ref, b_ref, r_ref, eig_ref, mu_ref,
     o_ref, hs_ref, hf_ref, low_ref,
 ):
     first = core_ref[0] == 0
@@ -195,7 +237,15 @@
     def put(at, tile, value):
         o_ref[at // 16 : (at + tile) // 16, 32:48, :] = value.reshape(tile // 16, 16, 256)
 
-    axial_solve(hs_ref, hf_ref, low_ref, a_ref, bt_ref, b_ref, r_ref, lam_ref, mu_ref, put)
+    b4 = b_ref.reshape(32, 2, 16, 1024)
+
+    def out_basis(at, tile):
+        return b4[at // 16 : (at + tile) // 16, core_ref[0]].reshape(tile, 1024)
+
+    axial_solve(
+        hs_ref, hf_ref, low_ref, a_ref, b_ref, out_basis,
+        r_ref, eig_ref, extra_ref[0], mu_ref, put, 512,
+    )
 
 
 def solve_scratch():
@@ -206,29 +256,29 @@
     ]
 
 
-def whole_call(lines, a, bt, b, r, lam, mu):
+def whole_call(chip, lines, a, b, r, eig, mu):
     return pl.pallas_call(
         whole_kernel,
-        in_specs=[vmem()] * 7,
+        in_specs=[smem()] + [vmem()] * 6,
         out_specs=vmem(),
         out_shape=jax.ShapeDtypeStruct((32, 32, 256), BF),
         scratch_shapes=solve_scratch(),
         compiler_params=pltpu.CompilerParams(vmem_limit_bytes=SOLVE_LIMIT),
         cost_estimate=pl.CostEstimate(flops=4 * 10**9, bytes_accessed=8 * 10**6, transcendentals=0),
         name="whole_pair",
-    )(lines, a, bt, b, r, lam, mu)
-
-
-def shared_call(core, own, other, whole, a, bt, b, r, lam, mu):
+    )(chip, lines, a, b, r, eig, mu)
+
+
+def shared_call(core, extra, own, other, whole, a, b, r, eig, mu):
     return pl.pallas_call(
         shared_kernel,
-        in_specs=[pl.BlockSpec(memory_space=pltpu.SMEM)] + [vmem()] * 9,
+        in_specs=[smem()] * 2 + [vmem()] * 8,
         out_specs=vmem(),
         out_shape=jax.ShapeDtypeStruct((32, 48, 256), BF),
         scratch_shapes=solve_scratch(),
         compiler_params=pltpu.CompilerParams(vmem_limit_bytes=SOLVE_LIMIT),
         name="shared_pair",
-    )(core, own, other, whole, a, bt, b, r, lam, mu)
+    )(core, extra, own, other, whole, a, b, r, eig, mu)
 
 
 def out_kernel(p_ref, o_ref):
@@ -273,37 +323,24 @@
     circle = velocity.shape[1] * row_total
     exchange = functools.partial(lax.all_to_all, split_axis=0, concat_axis=0, tiled=True)
 
-    fields = exchange(flux_call(velocity, adj_temp, radial_div), "row")
-
-    def pick(array, index):
-        return lax.dynamic_index_in_dim(array, index, 0, keepdims=False)
-
-    table = azimuth_table(mode_rows * row_total, circle, circle)
-    recip_half = lax.dynamic_slice_in_dim(reciprocal_distance, (row_place % 2) * 128, 128)
-    basis_turned = axial_basis.T
-    basis_half = pick(
-        axial_basis.reshape(col_total, 2, 16, axial_basis.shape[1]).swapaxes(0, 1), core
-    ).reshape(col_total * 16, axial_basis.shape[1])
-    shared_mode = 16 + jnp.minimum(chip, 2 * (mode_rows - 16) - 1) // 2
+    table = jnp.asarray(azimuth_table(mode_rows * row_total, circle, circle))
+    extra = (16 + jnp.minimum(chip, 2 * (mode_rows - 16) - 1) // 2).reshape(1)
+    core, half, chip = core.reshape(1), (row_place % 2).reshape(1), chip.reshape(1)
+    fields, whole_basis, shared_basis = flux_call(
+        chip, extra, velocity, adj_temp, radial_div, radial_basis
+    )
+    fields, core, half, table = lax.optimization_barrier((fields, core, half, table))
+    fields = exchange(fields, "row")
     mu = axial_eig[None, :]
-    whole_basis, shared_basis = pick(radial_basis, chip), pick(radial_basis, shared_mode)
-    whole_eig, shared_eig = pick(radial_eig, chip)[None, :], pick(radial_eig, shared_mode)[None, :]
-
-    later = [basis_turned, basis_half, whole_basis, shared_basis, whole_eig, shared_eig]
-    fields, later = lax.optimization_barrier((fields, later))
-    basis_turned, basis_half, whole_basis, shared_basis, whole_eig, shared_eig = later
-    spectra = spectra_call(fields, table, recip_half[None, :])
+    spectra = spectra_call(half, fields, table, reciprocal_distance[None, :])
     lines = exchange(spectra.reshape(row_total * col_total, 24, 128), ("row", "col"))
     lines = lines.reshape(row_total, col_total, 24, 128)
 
     own = lines[:, :, 16:24, :]
     other = lax.ppermute(own, "col", [(i, i ^ 1) for i in range(col_total)])
-    whole = whole_call(
-        lines, axial_diff, basis_turned, axial_basis, whole_basis, whole_eig, mu
-    )
+    whole = whole_call(chip, lines, axial_diff, axial_basis, whole_basis, radial_eig, mu)
     pieces = shared_call(
-        core.reshape(1), own, other, whole, axial_diff, basis_turned, basis_half,
-        shared_basis, shared_eig, mu,
+        core, extra, own, other, whole, axial_diff, axial_basis, shared_basis, radial_eig, mu
     )
     pieces = exchange(pieces, "col")
     return out_call(pieces.reshape(16, 2, 48, 256), mode_rows)

time: 141 us -> 149 us (1.057)
  blocking collectives: 82 us -> 126 us
  waiting for transfers between devices: 27.1 us -> 0.01 us
  local copies, waits for them, and re-layouts: 8.88 us -> 0.14 us
  Pallas kernels: 13.2 us -> 20.5 us
  starting transfers between devices: 7.95 us -> 1.58 us
    all_to_all x0 -> x1, blocking collectives: none -> 44.3 us  [body(): fields = exchange(fields, 'row')]
    all_to_all x1 -> x0, waiting for transfers between devices: 27.1 us -> none  [body(): fields = exchange(flux_call(velocity, adj_temp, radial_div), 'row')]
    pallas_call x4, Pallas kernels: 12 us -> 19.3 us  [the longest x1 11.8 us: flux_call(): pl.pallas_call(flux_kernel, grid=(nt // step,), in_specs=[smem(), smem(),...]
    all_to_all x1 -> x0, starting transfers between devices: 6.37 us -> none  [body(): fields = exchange(flux_call(velocity, adj_temp, radial_div), 'row')]
    unnamed x17 -> x16, local copies, waits for them, and re-layouts: 3.97 us -> 0.04 us
    another operation x1 -> x0, local copies, waits for them, and re-layouts: 2.32 us -> none
    squeeze x1 -> x0, local copies, waits for them, and re-layouts: 1.7 us -> none  [pick(): return lax.dynamic_index_in_dim(array, index, 0, keepdims=False)]
  transfers between devices with their start and end apart: 2 -> 1, of which waited for: 1 -> 0; matrix products, arithmetic and copies ran while one was open for 7% -> 0% of each run, Pallas kernels for 2% -> 2%
where the time goes in v4:
time: 149 us
  blocking collectives  126 us (85%)
  Pallas kernels  20.5 us (14%)
  starting transfers between devices  1.58 us (1%)
    all_to_all x1, blocking collectives, body(): exchange(spectra.reshape(row_total * col_total, 24, 128), ('row', 'col'))  54.8 us
    all_to_all x1, blocking collectives, body(): fields = exchange(fields, 'row')  44.3 us
    all_to_all x1, blocking collectives, body(): pieces = exchange(pieces, 'col')  27.1 us
    pallas_call x1, Pallas kernels, flux_call(): pl.pallas_call(flux_kernel, grid=(nt // step,), in_specs=[smem(), smem(),...  11.8 us
    pallas_call x1, Pallas kernels, whole_call(): pl.pallas_call(whole_kernel, in_specs=[smem()] + [vmem()] * 6, out_specs=...  3.08 us
  transfers between devices with their start and end apart: 1, of which 0 were waited for; matrix products, arithmetic and copies ran while one was open for 0% of the time, Pallas kernels for 2%

profile of v4, /device:TPU:1, one launch (start us, length us, event | category | flops | bytes accessed | tf_op | source)
XLA Modules:
  0.0 148.5 jit_solution(1899833877207964212)
XLA Ops:
  0.0 11.8 %flux.1 = (bf16[8,3,2,8,32,128]{5,4,3,2,1,0:T(8,128)(2,1)}, bf16[256,256]{1,0:T(8,128)(2,1)}, bf16[256,256]{1,0:T(8,128)(2,1)}) custom-call(s32[1]{0:T(128)} %bitcast.chip_ref, s32[1]{0:T(128)} %bitcast.1.extra_ref, bf16[3,64,32,256]{3,2,1,0:T(8,128)(2,1)} %v_ref.1, bf16[64,32,256]{2,1,0:T(8,128)(2,1)} %t_ref.1, bf16[256,256]{1,0:T(8,128)(2,1)} %d_ref.1, ...), custom_call_target="tpu_custom_call" | custom-call | tf_op jit(solution)/shard_map/flux/pallas_call | solution.py:83
  11.8 0.0 copy-start.2
  11.8 0.0 copy-start.6
  11.8 44.3 %all_to_all.15.x_ref = bf16[8,3,2,8,32,128]{5,4,3,2,1,0:T(8,128)(2,1)S(1)} all-to-all(bf16[8,3,2,8,32,128]{5,4,3,2,1,0:T(8,128)(2,1)} %get-tuple-element.15), channel_id=1, replica_groups=mesh['row'=8,'col'=32] {'row'}, dimensions={0} | all-to-all | bytes 6291456 | tf_op jit(solution)/shard_map/all_to_all | solution.py:333
  56.1 0.0 copy-done.2
  56.1 0.0 copy-done.6
  56.1 0.0 copy-start.4
  56.1 0.0 copy-start.7
  56.1 1.9 %spectra.1 = bf16[8,16,2,24,128]{4,3,2,1,0:T(8,128)(2,1)S(1)} custom-call(s32[1]{0:T(128)} %bitcast.3.half_ref, bf16[8,3,2,8,32,128]{5,4,3,2,1,0:T(8,128)(2,1)S(1)} %all_to_all.15.x_ref, bf16[336,512]{1,0:T(8,128)(2,1)S(1)} %copy-done.2, f32[1,256]{1,0:T(1,128)S(1)} %bitcast.15), custom_call_target="tpu_custom_call" | custom-call | tf_op jit(solution)/shard_map/spectra/pallas_call | solution.py:152
  58.0 0.0 copy-start
  58.0 0.0 copy-start.1
  58.0 0.0 copy-start.5
  58.1 54.8 %all_to_all.16 = bf16[256,24,128]{2,1,0:T(8,128)(2,1)S(1)} all-to-all(bf16[256,24,128]{2,1,0:T(8,128)(2,1)S(1)} %bitcast.9), channel_id=1, replica_groups=mesh['row'=8,'col'=32] {'row','col'}, dimensions={0} | all-to-all | bytes 3145728 | tf_op jit(solution)/shard_map/all_to_all | solution.py:336
  112.8 0.1 slice.4.own_ref
  112.9 1.6 %collective-permute-start = (bf16[8,32,8,128]{3,2,1,0:T(8,128)(2,1)S(1)}, bf16[8,32,8,128]{3,2,1,0:T(8,128)(2,1)S(1)}, u32[]{:S(2)}, u32[]{:S(2)}) collective-permute-start(bf16[8,32,8,128]{3,2,1,0:T(8,128)(2,1)S(1)} %slice.4.own_ref), channel_id=1, source_target_pairs={{0,1},{1,0},{2,3},{3,2},{4,5},{5,4},{6,7},{7,6},{8,9},{9,8},{10,11... | collective-permute-start | bytes 1572872 | tf_op jit(solution)/shard_map/ppermute | solution.py:340
  114.5 0.0 copy-done.4
  114.5 0.0 copy-done.7
  114.5 0.0 copy-done
  114.5 0.0 copy-done.1
  114.5 0.0 copy-done.5
  114.5 0.0 copy-start.3
  114.6 3.1 %whole_pair.1.whole_ref = bf16[32,32,256]{2,1,0:T(8,128)(2,1)S(1)} custom-call(s32[1]{0:T(128)} %bitcast.chip_ref, bf16[8,32,24,128]{3,2,1,0:T(8,128)(2,1)S(1)} %bitcast.12, bf16[1024,1024]{1,0:T(8,128)(2,1)S(1)} %copy-done, bf16[1024,1024]{1,0:T(8,128)(2,1)S(1)} %copy-done.1, bf16[256,256]{1,0:T(8,128)(2,1)S(1)} %copy-done.7, f32[21,256]{1,0:T(8,128)S(1)} %copy-done.4, ...), custom_call_target="tpu_custom_call" | custom-call | flops 4000000000 | bytes 8000000 | tf_op jit(solution)/shard_map/whole_pair/pallas_call | solution.py:260
  117.6 0.0 collective-permute-done.other_ref
  117.6 0.0 copy-done.3
  117.7 2.5 %shared_pair.1 = bf16[32,48,256]{2,1,0:T(8,128)(2,1)S(1)} custom-call(s32[1]{0:T(128)} %bitcast.2.core_ref, s32[1]{0:T(128)} %bitcast.1.extra_ref, bf16[8,32,8,128]{3,2,1,0:T(8,128)(2,1)S(1)} %slice.4.own_ref, bf16[8,32,8,128]{3,2,1,0:T(8,128)(2,1)S(1)} %collective-permute-done.other_ref, bf16[32,32,256]{2,1,0:T(8,128)(2,1)S(1)} %whole_pair.1.whole_ref, ...), custom_call_target="tpu_custom_call" | custom-call | tf_op jit(solution)/shard_map/shared_pair/pallas_call | solution.py:273
  120.2 27.1 %all_to_all.17 = bf16[32,48,256]{2,1,0:T(8,128)(2,1)S(1)} all-to-all(bf16[32,48,256]{2,1,0:T(8,128)(2,1)S(1)} %shared_pair.1), channel_id=1, replica_groups=mesh['row'=8,'col'=32] {'col'}, dimensions={0} | all-to-all | bytes 1572864 | tf_op jit(solution)/shard_map/all_to_all | solution.py:345
  147.4 1.2 result.1
Async XLA Ops:
  11.8 44.3 %copy-start.2 = (bf16[336,512]{1,0:T(8,128)(2,1)S(1)}, bf16[336,512]{1,0:T(8,128)(2,1)}, u32[]{:S(2)}) copy-start(bf16[336,512]{1,0:T(8,128)(2,1)} %constant.50.clone.w_ref) | copy-start | bytes 1032196
  11.8 44.3 %copy-start.6 = (f32[256]{0:T(256)S(1)}, f32[256]{0:T(256)}, u32[]{:S(2)}) copy-start(f32[256]{0:T(256)} %param.13) | copy-start | bytes 3076
  56.1 58.5 %copy-start.4 = (f32[21,256]{1,0:T(8,128)S(1)}, f32[21,256]{1,0:T(8,128)}, u32[]{:S(2)}) copy-start(f32[21,256]{1,0:T(8,128)} %eig_ref.3) | copy-start | bytes 64516
  56.1 58.5 %copy-start.7 = (bf16[256,256]{1,0:T(8,128)(2,1)S(1)}, bf16[256,256]{1,0:T(8,128)(2,1)}, u32[]{:S(2)}) copy-start(bf16[256,256]{1,0:T(8,128)(2,1)} %get-tuple-element.17.r_ref) | copy-start | bytes 393220
  58.0 56.5 %copy-start = (bf16[1024,1024]{1,0:T(8,128)(2,1)S(1)}, bf16[1024,1024]{1,0:T(8,128)(2,1)}, u32[]{:S(2)}) copy-start(bf16[1024,1024]{1,0:T(8,128)(2,1)} %a_ref.3) | copy-start | bytes 6291460
  58.0 56.5 %copy-start.1 = (bf16[1024,1024]{1,0:T(8,128)(2,1)S(1)}, bf16[1024,1024]{1,0:T(8,128)(2,1)}, u32[]{:S(2)}) copy-start(bf16[1024,1024]{1,0:T(8,128)(2,1)} %b_ref.3) | copy-start | bytes 6291460
  58.0 56.5 %copy-start.5 = (f32[1024]{0:T(1024)S(1)}, f32[1024]{0:T(1024)}, u32[]{:S(2)}) copy-start(f32[1024]{0:T(1024)} %param.18) | copy-start | bytes 12292
  112.9 4.7 %collective-permute-start = (bf16[8,32,8,128]{3,2,1,0:T(8,128)(2,1)S(1)}, bf16[8,32,8,128]{3,2,1,0:T(8,128)(2,1)S(1)}, u32[]{:S(2)}, u32[]{:S(2)}) collective-permute-start(bf16[8,32,8,128]{3,2,1,0:T(8,128)(2,1)S(1)} %slice.4.own_ref), channel_id=1, source_target_pairs={{0,1},{1,0},{2,3},{3,2},{4,5},{5,4},{6,7},{7,6},{8,9},{9,8},{10,11... | collective-permute-start | bytes 1572872 | tf_op jit(solution)/shard_map/ppermute | solution.py:340
  114.5 3.1 %copy-start.3 = (bf16[256,256]{1,0:T(8,128)(2,1)S(1)}, bf16[256,256]{1,0:T(8,128)(2,1)}, u32[]{:S(2)}) copy-start(bf16[256,256]{1,0:T(8,128)(2,1)} %get-tuple-element.18.r_ref) | copy-start | bytes 393220

commit v5 on v3

--- a/solution.py
+++ b/solution.py
@@ -40,7 +40,7 @@
         value = jnp.swapaxes(value, 0, 1).astype(BF)
         for group in range(4):
             for half in range(2):
-                x_ref[group * 2 + half, field, 0] = value[
+                x_ref[half * 4 + group, field, 0] = value[
                     group * 8 : group * 8 + 8, :, half * 128 : half * 128 + 128
                 ]
 
@@ -82,7 +82,12 @@
         def transform(field):
             columns = [
                 jnp.concatenate(
-                    [x_ref[s, field, h, z + k] for s in range(8) for h in range(2)], axis=0
+                    [
+                        x_ref[s % 2 * 4 + s // 2, field, h, z + k]
+                        for s in range(8)
+                        for h in range(2)
+                    ],
+                    axis=0,
                 )
                 for k in range(2)
             ]
@@ -153,6 +158,7 @@
 
 
 def whole_kernel(y_ref, a_ref, bt_ref, b_ref, r_ref, lam_ref, mu_ref, o_ref, hs_ref, hf_ref, low_ref):
+    slots = o_ref.reshape(4, 4, 2, 32, 256)
     hs4 = hs_ref.reshape(32, 4, 8, 256)
     hf4 = hf_ref.reshape(32, 4, 8, 256)
     for group in range(4):
@@ -164,7 +170,9 @@
         hf4[:, group] = hat[:, 1]
 
     def put(at, tile, value):
-        o_ref[at // 32 : (at + tile) // 32] = value.reshape(tile // 32, 32, 256)
+        value = value.reshape(tile // 256, 4, 2, 32, 256)
+        for x in range(tile // 256):
+            slots[:, at // 256 + x] = value[x]
 
     axial_solve(hs_ref, hf_ref, low_ref, a_ref, bt_ref, b_ref, r_ref, lam_ref, mu_ref, put)
 
@@ -174,6 +182,7 @@
     o_ref, hs_ref, hf_ref, low_ref,
 ):
     first = core_ref[0] == 0
+    slots = o_ref.reshape(4, 4, 2, 48, 256)
     hs4 = hs_ref.reshape(32, 4, 8, 256)
     hf4 = hf_ref.reshape(32, 4, 8, 256)
     for group in range(4):
@@ -193,7 +202,9 @@
     o_ref[:, 0:32, :] = whole_ref[...]
 
     def put(at, tile, value):
-        o_ref[at // 16 : (at + tile) // 16, 32:48, :] = value.reshape(tile // 16, 16, 256)
+        value = value.reshape(tile // 128, 4, 2, 16, 256)
+        for x in range(tile // 128):
+            slots[:, at // 128 + x, :, 32:48, :] = value[x]
 
     axial_solve(hs_ref, hf_ref, low_ref, a_ref, bt_ref, b_ref, r_ref, lam_ref, mu_ref, put)
 
@@ -232,12 +243,14 @@
 
 
 def out_kernel(p_ref, o_ref):
-    o_ref[0:16] = p_ref[:, :, 0:32, :].astype(F32)
+    for x in range(4):
+        o_ref[4 * x : 4 * x + 4] = p_ref[:, x, :, 0:32, :].astype(F32)
     for extra in range(o_ref.shape[0] - 16):
         for part in range(2):
+            chip = 2 * extra + part
             for core in range(2):
                 o_ref[16 + extra, part, 16 * core : 16 * core + 16, :] = p_ref[
-                    2 * extra + part, core, 32:48, :
+                    chip % 4, chip // 4, core, 32:48, :
                 ].astype(F32)
 
 
@@ -273,7 +286,11 @@
     circle = velocity.shape[1] * row_total
     exchange = functools.partial(lax.all_to_all, split_axis=0, concat_axis=0, tiled=True)
 
-    fields = exchange(flux_call(velocity, adj_temp, radial_div), "row")
+    row_order = [[y * 2 + low for low in range(2) for y in range(4)]]
+    col_order = [[x * 8 + z * 2 + c for z in range(4) for x in range(4) for c in range(2)]]
+    fields = exchange(
+        flux_call(velocity, adj_temp, radial_div), "row", axis_index_groups=row_order
+    )
 
     def pick(array, index):
         return lax.dynamic_index_in_dim(array, index, 0, keepdims=False)
@@ -305,8 +322,8 @@
         core.reshape(1), own, other, whole, axial_diff, basis_turned, basis_half,
         shared_basis, shared_eig, mu,
     )
-    pieces = exchange(pieces, "col")
-    return out_call(pieces.reshape(16, 2, 48, 256), mode_rows)
+    pieces = exchange(pieces, "col", axis_index_groups=col_order)
+    return out_call(pieces.reshape(4, 4, 2, 48, 256), mode_rows)
 
 
 def solution(mesh):

time: 141 us -> 140 us (level)
  no operation moved by 1% of the time
where the time goes in v5:
time: 140 us
  blocking collectives  80.8 us (58%)
  waiting for transfers between devices  27.2 us (19%)
  Pallas kernels  13.2 us (9%)
  local copies, waits for them, and re-layouts  8.88 us (6%)
  starting transfers between devices  7.95 us (6%)
  other arithmetic  1.46 us (1%)
    all_to_all x1, blocking collectives, body(): exchange(spectra.reshape(row_total * col_total, 24, 128), ('row', 'col'))  54.6 us
    all_to_all x1, waiting for transfers between devices, body(): exchange(flux_call(velocity, adj_temp, radial_div), 'row', axis_index_gro...  27.2 us
    all_to_all x1, blocking collectives, body(): pieces = exchange(pieces, 'col', axis_index_groups=col_order)  26.2 us
    all_to_all x1, starting transfers between devices, body(): exchange(flux_call(velocity, adj_temp, radial_div), 'row', axis_index_gro...  6.37 us
    pallas_call x1, Pallas kernels, flux_call(): pl.pallas_call(flux_kernel, grid=(nt // step,), in_specs=[pl.BlockSpec((3...  4.65 us
    unnamed x17, local copies, waits for them, and re-layouts  3.97 us
    pallas_call x1, Pallas kernels, whole_call(): pl.pallas_call(whole_kernel, in_specs=[vmem()] * 7, out_specs=vmem(), out...  3 us
  transfers between devices with their start and end apart: 2, of which 1 were waited for; matrix products, arithmetic and copies ran while one was open for 7% of the time, Pallas kernels for 2%

profile of v5, /device:TPU:1, one launch (start us, length us, event | category | flops | bytes accessed | tf_op | source)
XLA Modules:
  0.0 139.5 jit_solution(2191000261133645998)
XLA Ops:
  0.0 0.0 copy-start
  0.0 4.7 %flux.1 = bf16[8,3,2,8,32,128]{5,4,3,2,1,0:T(8,128)(2,1)} custom-call(bf16[3,64,32,256]{3,2,1,0:T(8,128)(2,1)} %v_ref.1, bf16[64,32,256]{2,1,0:T(8,128)(2,1)} %t_ref.1, bf16[256,256]{1,0:T(8,128)(2,1)} %d_ref.1), custom_call_target="tpu_custom_call" | custom-call | tf_op jit(solution)/shard_map/flux/pallas_call | solution.py:57
  4.7 6.4 %all-to-all-start = ((bf16[8,3,2,8,32,128]{5,4,3,2,1,0:T(8,128)(2,1)}), bf16[8,3,2,8,32,128]{5,4,3,2,1,0:T(8,128)(2,1)S(1)}, u32[]{:S(2)}, u32[]{:S(2)}) async-start(bf16[8,3,2,8,32,128]{5,4,3,2,1,0:T(8,128)(2,1)} %flux.1), calls=%async_computation | async-start | bytes 6291456 | tf_op jit(solution)/shard_map/all_to_all | solution.py:291
  11.0 3.9 %copy.10 = bf16[1024,1024]{0,1:T(8,128)(2,1)} copy(bf16[1024,1024]{1,0:T(8,128)(2,1)} %b_ref.1) | data formatting | bytes 4194304 | tf_op args[7]
  15.0 0.0 copy-done
  15.0 0.1 dynamic-slice_bitcast_fusion.2.recip_ref
  15.0 0.7 constant_dynamic-slice_fusion
  15.8 1.7 %dynamic-slice_bitcast_fusion = (bf16[256,256]{1,0:T(8,128)(2,1)}, bf16[256,256]{1,0:T(8,128)(2,1)}) fusion(bf16[21,256,256]{2,1,0:T(8,128)(2,1)} %param.13, s32[]{:T(128)S(6)} %select_n.48, s32[]{:T(128)S(6)} %select_n.46), kind=kLoop, calls=%fused_computation.12 | loop fusion | bytes 524296 | tf_op jit(solution)/shard_map/jit(dynamic_index_in_dim)/squeeze | solution.py:296
  17.5 1.4 %multiply_convert_fusion = (bf16[168,512]{1,0:T(8,128)(2,1)S(1)}, bf16[168,512]{1,0:T(8,128)(2,1)S(1)}) fusion(), kind=kLoop, calls=%fused_computation.7 | loop fusion | flops 1634304 | bytes 344064 | tf_op jit(solution)/shard_map/convert.1
  18.9 2.3 %constant_dynamic-slice_fusion.2 = bf16[32,1,16,1024]{3,2,1,0:T(8,128)(2,1)} fusion(bf16[32,2,16,1024]{3,2,1,0:T(8,128)(2,1)} %bitcast.19, s32[]{:T(128)S(6)} %select_n.44), kind=kLoop, calls=%fused_computation.16 | loop fusion | bytes 2097156 | tf_op jit(solution)/shard_map/dynamic-slice
  21.3 27.2 %all-to-all-done.x_ref = bf16[8,3,2,8,32,128]{5,4,3,2,1,0:T(8,128)(2,1)S(1)} async-done(((bf16[8,3,2,8,32,128]{5,4,3,2,1,0:T(8,128)(2,1)}), bf16[8,3,2,8,32,128]{5,4,3,2,1,0:T(8,128)(2,1)S(1)}, u32[]{:S(2)}, u32[]{:S(2)}) %all-to-all-start) | async-done | bytes 3145760 | tf_op jit(solution)/shard_map/all_to_all | solution.py:291
  48.4 0.0 copy-start.4
  48.4 2.0 %spectra.1 = bf16[8,16,2,24,128]{4,3,2,1,0:T(8,128)(2,1)S(1)} custom-call(bf16[8,3,2,8,32,128]{5,4,3,2,1,0:T(8,128)(2,1)S(1)} %all-to-all-done.x_ref, bf16[336,512]{1,0:T(8,128)(2,1)S(1)} %pad_maximum_fusion.w_ref, f32[1,128]{1,0:T(1,128)S(1)} %dynamic-slice_bitcast_fusion.2.recip_ref), custom_call_target="tpu_custom_call" | custom-call | tf_op jit(solution)/shard_map/spectra/pallas_call | solution.py:123
  50.4 0.0 copy-start.1
  50.4 0.0 copy-start.2
  50.4 54.6 %all_to_all.15 = bf16[256,24,128]{2,1,0:T(8,128)(2,1)S(1)} all-to-all(bf16[256,24,128]{2,1,0:T(8,128)(2,1)S(1)} %bitcast.18), channel_id=1, replica_groups=mesh['row'=8,'col'=32] {'row','col'}, dimensions={0} | all-to-all | bytes 3145728 | tf_op jit(solution)/shard_map/all_to_all | solution.py:313
  105.0 0.1 slice.4.own_ref
  105.1 1.6 %collective-permute-start = (bf16[8,32,8,128]{3,2,1,0:T(8,128)(2,1)S(1)}, bf16[8,32,8,128]{3,2,1,0:T(8,128)(2,1)S(1)}, u32[]{:S(2)}, u32[]{:S(2)}) collective-permute-start(bf16[8,32,8,128]{3,2,1,0:T(8,128)(2,1)S(1)} %slice.4.own_ref), channel_id=1, source_target_pairs={{0,1},{1,0},{2,3},{3,2},{4,5},{5,4},{6,7},{7,6},{8,9},{9,8},{10,11... | collective-permute-start | bytes 1572872 | tf_op jit(solution)/shard_map/ppermute | solution.py:317
  106.7 0.0 copy-done.4
  106.7 0.0 copy-done.6
  106.7 0.0 copy-done.7
  106.7 0.0 copy-done.1
  106.7 0.0 copy-done.2
  106.7 0.0 copy-start.3
  106.7 0.0 copy-start.5
  106.7 3.0 %whole_pair.1.whole_ref = bf16[32,32,256]{2,1,0:T(8,128)(2,1)S(1)} custom-call(bf16[8,32,24,128]{3,2,1,0:T(8,128)(2,1)S(1)} %bitcast.23, bf16[1024,1024]{1,0:T(8,128)(2,1)S(1)} %copy-done.4, bf16[1024,1024]{1,0:T(8,128)(2,1)S(1)} %bitcast.16, bf16[1024,1024]{1,0:T(8,128)(2,1)S(1)} %copy-done.2, bf16[256,256]{1,0:T(8,128)(2,1)S(1)} %copy-done.6, ...), custom_call_target="tpu_custom_call" | custom-call | flops 4000000000 | bytes 8000000 | tf_op jit(solution)/shard_map/whole_pair/pallas_call | solution.py:221
  109.7 0.0 collective-permute-done.other_ref
  109.7 0.0 copy-done.3
  109.7 0.0 copy-done.5
  109.7 2.4 %shared_pair.1 = bf16[32,48,256]{2,1,0:T(8,128)(2,1)S(1)} custom-call(s32[1]{0:T(128)} %bitcast.core_ref, bf16[8,32,8,128]{3,2,1,0:T(8,128)(2,1)S(1)} %slice.4.own_ref, bf16[8,32,8,128]{3,2,1,0:T(8,128)(2,1)S(1)} %collective-permute-done.other_ref, bf16[32,32,256]{2,1,0:T(8,128)(2,1)S(1)} %whole_pair.1.whole_ref, bf16[1024,1024]{1,0:T(8,128)(2,1)S(1)} %copy-done.4, ...), custom_call_target="tpu_custom_call" | custom-call | tf_op jit(solution)/shard_map/shared_pair/pallas_call | solution.py:234
  112.1 26.2 %all_to_all.16 = bf16[32,48,256]{2,1,0:T(8,128)(2,1)S(1)} all-to-all(bf16[32,48,256]{2,1,0:T(8,128)(2,1)S(1)} %shared_pair.1), channel_id=1, replica_groups={{0,1,8,9,16,17,24,25,2,3,10,11,18,19,26,27,4,5,12,13,20,21,28,29,6,7,14..., dimensions={0} | all-to-all | bytes 1572864 | tf_op jit(solution)/shard_map/all_to_all | solution.py:325
  138.3 1.2 result.1
  (3 shorter events, 0.0 us)
Async XLA Ops:
  0.0 15.0 %copy-start = (f32[256]{0:T(256)S(1)}, f32[256]{0:T(256)}, u32[]{:S(2)}) copy-start(f32[256]{0:T(256)} %param.12) | copy-start | bytes 3076
  4.7 43.8 %all-to-all-start = ((bf16[8,3,2,8,32,128]{5,4,3,2,1,0:T(8,128)(2,1)}), bf16[8,3,2,8,32,128]{5,4,3,2,1,0:T(8,128)(2,1)S(1)}, u32[]{:S(2)}, u32[]{:S(2)}) async-start(bf16[8,3,2,8,32,128]{5,4,3,2,1,0:T(8,128)(2,1)} %flux.1), calls=%async_computation | async-start | bytes 6291456 | tf_op jit(solution)/shard_map/all_to_all | solution.py:291
  48.4 58.2 %copy-start.4 = (bf16[1024,1024]{1,0:T(8,128)(2,1)S(1)}, bf16[1024,1024]{1,0:T(8,128)(2,1)}, u32[]{:S(2)}) copy-start(bf16[1024,1024]{1,0:T(8,128)(2,1)} %a_ref.3) | copy-start | bytes 6291460
  48.4 58.3 %copy-start.6 = (bf16[256,256]{1,0:T(8,128)(2,1)S(1)}, bf16[256,256]{1,0:T(8,128)(2,1)}, u32[]{:S(2)}) copy-start(bf16[256,256]{1,0:T(8,128)(2,1)} %get-tuple-element.14.r_ref) | copy-start | bytes 393220
  48.4 58.3 %copy-start.7 = (f32[1024]{0:T(1024)S(1)}, f32[1024]{0:T(1024)}, u32[]{:S(2)}) copy-start(f32[1024]{0:T(1024)} %param.17) | copy-start | bytes 12292
  50.4 56.3 %copy-start.1 = (bf16[1024,1024]{0,1:T(8,128)(2,1)S(1)}, bf16[1024,1024]{0,1:T(8,128)(2,1)}, u32[]{:S(2)}) copy-start(bf16[1024,1024]{0,1:T(8,128)(2,1)} %copy.10) | copy-start | bytes 6291460
  50.4 56.3 %copy-start.2 = (bf16[1024,1024]{1,0:T(8,128)(2,1)S(1)}, bf16[1024,1024]{1,0:T(8,128)(2,1)}, u32[]{:S(2)}) copy-start(bf16[1024,1024]{1,0:T(8,128)(2,1)} %b_ref.1) | copy-start | bytes 6291460
  105.1 4.6 %collective-permute-start = (bf16[8,32,8,128]{3,2,1,0:T(8,128)(2,1)S(1)}, bf16[8,32,8,128]{3,2,1,0:T(8,128)(2,1)S(1)}, u32[]{:S(2)}, u32[]{:S(2)}) collective-permute-start(bf16[8,32,8,128]{3,2,1,0:T(8,128)(2,1)S(1)} %slice.4.own_ref), channel_id=1, source_target_pairs={{0,1},{1,0},{2,3},{3,2},{4,5},{5,4},{6,7},{7,6},{8,9},{9,8},{10,11... | collective-permute-start | bytes 1572872 | tf_op jit(solution)/shard_map/ppermute | solution.py:317
  106.7 3.0 %copy-start.3 = (bf16[32,1,16,1024]{3,2,1,0:T(8,128)(2,1)S(1)}, bf16[32,1,16,1024]{3,2,1,0:T(8,128)(2,1)}, u32[]{:S(2)}) copy-start(bf16[32,1,16,1024]{3,2,1,0:T(8,128)(2,1)} %constant_dynamic-slice_fusion.2) | copy-start | bytes 3145732
  106.7 3.0 %copy-start.5 = (bf16[256,256]{1,0:T(8,128)(2,1)S(1)}, bf16[256,256]{1,0:T(8,128)(2,1)}, u32[]{:S(2)}) copy-start(bf16[256,256]{1,0:T(8,128)(2,1)} %get-tuple-element.17.r_ref) | copy-start | bytes 393220

commit v6 on v5

--- a/solution.py
+++ b/solution.py
@@ -76,8 +76,8 @@
     mode_id = lax.broadcasted_iota(jnp.int32, (modes, 128), 0).astype(F32)
     scale = mode_id * recip_ref[...]
     scale = jnp.concatenate([scale, scale], axis=0)
-    scale = jnp.concatenate([scale, scale], axis=1)
-    for z in range(0, 8, 2):
+    scale = jnp.concatenate([scale] * 4, axis=1)
+    for z in range(0, 8, 4):
 
         def transform(field):
             columns = [
@@ -89,7 +89,7 @@
                     ],
                     axis=0,
                 )
-                for k in range(2)
+                for k in range(4)
             ]
             return jnp.dot(
                 table, jnp.concatenate(columns, axis=1), preferred_element_type=F32
@@ -99,7 +99,7 @@
         turned = jnp.concatenate([-angular[modes:], angular[:modes]], axis=0)
         source = transform(0) + scale * turned
         axial = transform(2)
-        for k in range(2):
+        for k in range(4):
             lanes = slice(k * 128, k * 128 + 128)
             u_ref[pl.ds(z + k, rows, stride=16), :] = source[:, lanes]
             u_ref[pl.ds(8 + z + k, rows, stride=16), :] = axial[:, lanes]

time: 140 us -> 140 us (level)
  no operation moved by 1% of the time
where the time goes in v6:
time: 140 us; the launch traced here: 139 us
  blocking collectives  80.8 us (58%)
  waiting for transfers between devices  27.2 us (19%)
  Pallas kernels  13.1 us (9%)
  local copies, waits for them, and re-layouts  8.88 us (6%)
  starting transfers between devices  7.95 us (6%)
  other arithmetic  1.46 us (1%)
    all_to_all x1, blocking collectives, body(): exchange(spectra.reshape(row_total * col_total, 24, 128), ('row', 'col'))  54.6 us
    all_to_all x1, waiting for transfers between devices, body(): exchange(flux_call(velocity, adj_temp, radial_div), 'row', axis_index_gro...  27.2 us
    all_to_all x1, blocking collectives, body(): pieces = exchange(pieces, 'col', axis_index_groups=col_order)  26.2 us
    all_to_all x1, starting transfers between devices, body(): exchange(flux_call(velocity, adj_temp, radial_div), 'row', axis_index_gro...  6.37 us
    pallas_call x1, Pallas kernels, flux_call(): pl.pallas_call(flux_kernel, grid=(nt // step,), in_specs=[pl.BlockSpec((3...  4.65 us
    unnamed x17, local copies, waits for them, and re-layouts  3.97 us
    pallas_call x1, Pallas kernels, whole_call(): pl.pallas_call(whole_kernel, in_specs=[vmem()] * 7, out_specs=vmem(), out...  3.01 us
  transfers between devices with their start and end apart: 2, of which 1 were waited for; matrix products, arithmetic and copies ran while one was open for 7% of the time, Pallas kernels for 2%

profile of v6, /device:TPU:1, one launch (start us, length us, event | category | flops | bytes accessed | tf_op | source)
XLA Modules:
  0.0 139.4 jit_solution(9106357367699775439)
XLA Ops:
  0.0 0.0 copy-start
  0.0 4.7 %flux.1 = bf16[8,3,2,8,32,128]{5,4,3,2,1,0:T(8,128)(2,1)} custom-call(bf16[3,64,32,256]{3,2,1,0:T(8,128)(2,1)} %v_ref.1, bf16[64,32,256]{2,1,0:T(8,128)(2,1)} %t_ref.1, bf16[256,256]{1,0:T(8,128)(2,1)} %d_ref.1), custom_call_target="tpu_custom_call" | custom-call | tf_op jit(solution)/shard_map/flux/pallas_call | solution.py:57
  4.7 6.4 %all-to-all-start = ((bf16[8,3,2,8,32,128]{5,4,3,2,1,0:T(8,128)(2,1)}), bf16[8,3,2,8,32,128]{5,4,3,2,1,0:T(8,128)(2,1)S(1)}, u32[]{:S(2)}, u32[]{:S(2)}) async-start(bf16[8,3,2,8,32,128]{5,4,3,2,1,0:T(8,128)(2,1)} %flux.1), calls=%async_computation | async-start | bytes 6291456 | tf_op jit(solution)/shard_map/all_to_all | solution.py:291
  11.0 3.9 %copy.10 = bf16[1024,1024]{0,1:T(8,128)(2,1)} copy(bf16[1024,1024]{1,0:T(8,128)(2,1)} %b_ref.1) | data formatting | bytes 4194304 | tf_op args[7]
  15.0 0.0 copy-done
  15.0 0.1 dynamic-slice_bitcast_fusion.2.recip_ref
  15.0 0.7 constant_dynamic-slice_fusion
  15.8 1.7 %dynamic-slice_bitcast_fusion = (bf16[256,256]{1,0:T(8,128)(2,1)}, bf16[256,256]{1,0:T(8,128)(2,1)}) fusion(bf16[21,256,256]{2,1,0:T(8,128)(2,1)} %param.13, s32[]{:T(128)S(6)} %select_n.48, s32[]{:T(128)S(6)} %select_n.46), kind=kLoop, calls=%fused_computation.12 | loop fusion | bytes 524296 | tf_op jit(solution)/shard_map/jit(dynamic_index_in_dim)/squeeze | solution.py:296
  17.5 1.4 %multiply_convert_fusion = (bf16[168,512]{1,0:T(8,128)(2,1)S(1)}, bf16[168,512]{1,0:T(8,128)(2,1)S(1)}) fusion(), kind=kLoop, calls=%fused_computation.7 | loop fusion | flops 1634304 | bytes 344064 | tf_op jit(solution)/shard_map/convert.1
  18.9 2.3 %constant_dynamic-slice_fusion.2 = bf16[32,1,16,1024]{3,2,1,0:T(8,128)(2,1)} fusion(bf16[32,2,16,1024]{3,2,1,0:T(8,128)(2,1)} %bitcast.19, s32[]{:T(128)S(6)} %select_n.44), kind=kLoop, calls=%fused_computation.16 | loop fusion | bytes 2097156 | tf_op jit(solution)/shard_map/dynamic-slice
  21.3 27.2 %all-to-all-done.x_ref = bf16[8,3,2,8,32,128]{5,4,3,2,1,0:T(8,128)(2,1)S(1)} async-done(((bf16[8,3,2,8,32,128]{5,4,3,2,1,0:T(8,128)(2,1)}), bf16[8,3,2,8,32,128]{5,4,3,2,1,0:T(8,128)(2,1)S(1)}, u32[]{:S(2)}, u32[]{:S(2)}) %all-to-all-start) | async-done | bytes 3145760 | tf_op jit(solution)/shard_map/all_to_all | solution.py:291
  48.4 0.0 copy-start.4
  48.4 1.9 %spectra.1 = bf16[8,16,2,24,128]{4,3,2,1,0:T(8,128)(2,1)S(1)} custom-call(bf16[8,3,2,8,32,128]{5,4,3,2,1,0:T(8,128)(2,1)S(1)} %all-to-all-done.x_ref, bf16[336,512]{1,0:T(8,128)(2,1)S(1)} %pad_maximum_fusion.w_ref, f32[1,128]{1,0:T(1,128)S(1)} %dynamic-slice_bitcast_fusion.2.recip_ref), custom_call_target="tpu_custom_call" | custom-call | tf_op jit(solution)/shard_map/spectra/pallas_call | solution.py:123
  50.3 0.0 copy-start.1
  50.3 0.0 copy-start.2
  50.3 54.6 %all_to_all.15 = bf16[256,24,128]{2,1,0:T(8,128)(2,1)S(1)} all-to-all(bf16[256,24,128]{2,1,0:T(8,128)(2,1)S(1)} %bitcast.18), channel_id=1, replica_groups=mesh['row'=8,'col'=32] {'row','col'}, dimensions={0} | all-to-all | bytes 3145728 | tf_op jit(solution)/shard_map/all_to_all | solution.py:313
  104.9 0.1 slice.4.own_ref
  105.0 1.6 %collective-permute-start = (bf16[8,32,8,128]{3,2,1,0:T(8,128)(2,1)S(1)}, bf16[8,32,8,128]{3,2,1,0:T(8,128)(2,1)S(1)}, u32[]{:S(2)}, u32[]{:S(2)}) collective-permute-start(bf16[8,32,8,128]{3,2,1,0:T(8,128)(2,1)S(1)} %slice.4.own_ref), channel_id=1, source_target_pairs={{0,1},{1,0},{2,3},{3,2},{4,5},{5,4},{6,7},{7,6},{8,9},{9,8},{10,11... | collective-permute-start | bytes 1572872 | tf_op jit(solution)/shard_map/ppermute | solution.py:317
  106.6 0.0 copy-done.4
  106.6 0.0 copy-done.6
  106.6 0.0 copy-done.7
  106.6 0.0 copy-done.1
  106.6 0.0 copy-done.2
  106.6 0.0 copy-start.3
  106.6 0.0 copy-start.5
  106.6 3.0 %whole_pair.1.whole_ref = bf16[32,32,256]{2,1,0:T(8,128)(2,1)S(1)} custom-call(bf16[8,32,24,128]{3,2,1,0:T(8,128)(2,1)S(1)} %bitcast.23, bf16[1024,1024]{1,0:T(8,128)(2,1)S(1)} %copy-done.4, bf16[1024,1024]{1,0:T(8,128)(2,1)S(1)} %bitcast.16, bf16[1024,1024]{1,0:T(8,128)(2,1)S(1)} %copy-done.2, bf16[256,256]{1,0:T(8,128)(2,1)S(1)} %copy-done.6, ...), custom_call_target="tpu_custom_call" | custom-call | flops 4000000000 | bytes 8000000 | tf_op jit(solution)/shard_map/whole_pair/pallas_call | solution.py:221
  109.6 0.0 collective-permute-done.other_ref
  109.6 0.0 copy-done.3
  109.6 0.0 copy-done.5
  109.6 2.4 %shared_pair.1 = bf16[32,48,256]{2,1,0:T(8,128)(2,1)S(1)} custom-call(s32[1]{0:T(128)} %bitcast.core_ref, bf16[8,32,8,128]{3,2,1,0:T(8,128)(2,1)S(1)} %slice.4.own_ref, bf16[8,32,8,128]{3,2,1,0:T(8,128)(2,1)S(1)} %collective-permute-done.other_ref, bf16[32,32,256]{2,1,0:T(8,128)(2,1)S(1)} %whole_pair.1.whole_ref, bf16[1024,1024]{1,0:T(8,128)(2,1)S(1)} %copy-done.4, ...), custom_call_target="tpu_custom_call" | custom-call | tf_op jit(solution)/shard_map/shared_pair/pallas_call | solution.py:234
  112.1 26.2 %all_to_all.16 = bf16[32,48,256]{2,1,0:T(8,128)(2,1)S(1)} all-to-all(bf16[32,48,256]{2,1,0:T(8,128)(2,1)S(1)} %shared_pair.1), channel_id=1, replica_groups={{0,1,8,9,16,17,24,25,2,3,10,11,18,19,26,27,4,5,12,13,20,21,28,29,6,7,14..., dimensions={0} | all-to-all | bytes 1572864 | tf_op jit(solution)/shard_map/all_to_all | solution.py:325
  138.3 1.2 result.1
  (3 shorter events, 0.0 us)
Async XLA Ops:
  0.0 15.0 %copy-start = (f32[256]{0:T(256)S(1)}, f32[256]{0:T(256)}, u32[]{:S(2)}) copy-start(f32[256]{0:T(256)} %param.12) | copy-start | bytes 3076
  4.7 43.8 %all-to-all-start = ((bf16[8,3,2,8,32,128]{5,4,3,2,1,0:T(8,128)(2,1)}), bf16[8,3,2,8,32,128]{5,4,3,2,1,0:T(8,128)(2,1)S(1)}, u32[]{:S(2)}, u32[]{:S(2)}) async-start(bf16[8,3,2,8,32,128]{5,4,3,2,1,0:T(8,128)(2,1)} %flux.1), calls=%async_computation | async-start | bytes 6291456 | tf_op jit(solution)/shard_map/all_to_all | solution.py:291
  48.4 58.2 %copy-start.4 = (bf16[1024,1024]{1,0:T(8,128)(2,1)S(1)}, bf16[1024,1024]{1,0:T(8,128)(2,1)}, u32[]{:S(2)}) copy-start(bf16[1024,1024]{1,0:T(8,128)(2,1)} %a_ref.3) | copy-start | bytes 6291460
  48.4 58.2 %copy-start.6 = (bf16[256,256]{1,0:T(8,128)(2,1)S(1)}, bf16[256,256]{1,0:T(8,128)(2,1)}, u32[]{:S(2)}) copy-start(bf16[256,256]{1,0:T(8,128)(2,1)} %get-tuple-element.14.r_ref) | copy-start | bytes 393220
  48.4 58.2 %copy-start.7 = (f32[1024]{0:T(1024)S(1)}, f32[1024]{0:T(1024)}, u32[]{:S(2)}) copy-start(f32[1024]{0:T(1024)} %param.17) | copy-start | bytes 12292
  50.3 56.3 %copy-start.1 = (bf16[1024,1024]{0,1:T(8,128)(2,1)S(1)}, bf16[1024,1024]{0,1:T(8,128)(2,1)}, u32[]{:S(2)}) copy-start(bf16[1024,1024]{0,1:T(8,128)(2,1)} %copy.10) | copy-start | bytes 6291460
  50.3 56.3 %copy-start.2 = (bf16[1024,1024]{1,0:T(8,128)(2,1)S(1)}, bf16[1024,1024]{1,0:T(8,128)(2,1)}, u32[]{:S(2)}) copy-start(bf16[1024,1024]{1,0:T(8,128)(2,1)} %b_ref.1) | copy-start | bytes 6291460
  105.0 4.6 %collective-permute-start = (bf16[8,32,8,128]{3,2,1,0:T(8,128)(2,1)S(1)}, bf16[8,32,8,128]{3,2,1,0:T(8,128)(2,1)S(1)}, u32[]{:S(2)}, u32[]{:S(2)}) collective-permute-start(bf16[8,32,8,128]{3,2,1,0:T(8,128)(2,1)S(1)} %slice.4.own_ref), channel_id=1, source_target_pairs={{0,1},{1,0},{2,3},{3,2},{4,5},{5,4},{6,7},{7,6},{8,9},{9,8},{10,11... | collective-permute-start | bytes 1572872 | tf_op jit(solution)/shard_map/ppermute | solution.py:317
  106.6 3.0 %copy-start.3 = (bf16[32,1,16,1024]{3,2,1,0:T(8,128)(2,1)S(1)}, bf16[32,1,16,1024]{3,2,1,0:T(8,128)(2,1)}, u32[]{:S(2)}) copy-start(bf16[32,1,16,1024]{3,2,1,0:T(8,128)(2,1)} %constant_dynamic-slice_fusion.2) | copy-start | bytes 3145732
  106.6 3.0 %copy-start.5 = (bf16[256,256]{1,0:T(8,128)(2,1)S(1)}, bf16[256,256]{1,0:T(8,128)(2,1)}, u32[]{:S(2)}) copy-start(bf16[256,256]{1,0:T(8,128)(2,1)} %get-tuple-element.17.r_ref) | copy-start | bytes 393220

commit v7 on v6

--- a/solution.py
+++ b/solution.py
@@ -108,15 +108,15 @@
         for part in range(2):
             first = (part * modes + row * block) * 16
             mine = u_ref[first : first + 16 * 16, :].reshape(16, 16, 128)
-            y_ref[row, :, part, 0:16, :] = mine.astype(BF)
+            y_ref[:, part, row, 0:16, :] = mine.astype(BF)
             for extra in range(block - 16):
                 at = first + (16 + extra) * 16
                 for core in range(2):
-                    y_ref[row, 2 * extra + part, core, 16:24, :] = u_ref[
+                    y_ref[2 * extra + part, core, row, 16:24, :] = u_ref[
                         at + 8 * core : at + 8 * core + 8, :
                     ].astype(BF)
         for chip in range(2 * (block - 16), 16):
-            y_ref[row, chip, :, 16:24, :] = jnp.zeros((2, 8, 128), BF)
+            y_ref[chip, :, row, 16:24, :] = jnp.zeros((2, 8, 128), BF)
 
 
 def spectra_call(fields, table, recip_half):
@@ -124,7 +124,7 @@
         spectra_kernel,
         in_specs=[vmem()] * 3,
         out_specs=vmem(),
-        out_shape=jax.ShapeDtypeStruct((8, 16, 2, 24, 128), BF),
+        out_shape=jax.ShapeDtypeStruct((16, 2, 8, 24, 128), BF),
         scratch_shapes=[pltpu.VMEM((table.shape[0] * 16 + 16, 128), F32)],
         compiler_params=pltpu.CompilerParams(vmem_limit_bytes=SPECTRA_LIMIT),
         name="spectra",
@@ -163,7 +163,7 @@
     hf4 = hf_ref.reshape(32, 4, 8, 256)
     for group in range(4):
         left = jnp.concatenate(
-            [y_ref[2 * group + half, :, 0:16, :].reshape(512, 128) for half in range(2)], axis=1
+            [y_ref[:, 2 * group + half, 0:16, :].reshape(512, 128) for half in range(2)], axis=1
         )
         hat = jnp.dot(left, r_ref[...], preferred_element_type=F32).reshape(32, 2, 8, 256)
         hs4[:, group] = hat[:, 0]
@@ -189,7 +189,7 @@
 
         def hat(ref):
             left = jnp.concatenate(
-                [ref[2 * group + half].astype(F32).reshape(256, 128) for half in range(2)], axis=1
+                [ref[:, 2 * group + half].astype(F32).reshape(256, 128) for half in range(2)], axis=1
             )
             return jnp.dot(
                 left.astype(BF), r_ref[...], preferred_element_type=F32
@@ -310,8 +310,8 @@
     fields, later = lax.optimization_barrier((fields, later))
     basis_turned, basis_half, whole_basis, shared_basis, whole_eig, shared_eig = later
     spectra = spectra_call(fields, table, recip_half[None, :])
-    lines = exchange(spectra.reshape(row_total * col_total, 24, 128), ("row", "col"))
-    lines = lines.reshape(row_total, col_total, 24, 128)
+    lines = exchange(spectra.reshape(row_total * col_total, 24, 128), ("col", "row"))
+    lines = lines.reshape(col_total, row_total, 24, 128)
 
     own = lines[:, :, 16:24, :]
     other = lax.ppermute(own, "col", [(i, i ^ 1) for i in range(col_total)])

time: 140 us -> 140 us (level); the launches traced: 139 us -> 138 us
  starting transfers between devices: 7.95 us -> 6.46 us
    all_to_all x1, blocking collectives: 26.2 us -> 24.5 us  [body(): pieces = exchange(pieces, 'col', axis_index_groups=col_order)]
    ppermute x1, starting transfers between devices: 1.58 us -> 0.09 us  [body(): other = lax.ppermute(own, 'col', [(i, i ^ 1) for i in range(col_total)])]
where the time goes in v7:
time: 140 us; the launch traced here: 138 us
  blocking collectives  80.2 us (57%)
  waiting for transfers between devices  27.2 us (19%)
  Pallas kernels  13.2 us (9%)
  local copies, waits for them, and re-layouts  8.88 us (6%)
  starting transfers between devices  6.46 us (5%)
  other arithmetic  1.46 us (1%)
    all_to_all x1, blocking collectives, body(): exchange(spectra.reshape(row_total * col_total, 24, 128), ('col', 'row'))  55.7 us
    all_to_all x1, waiting for transfers between devices, body(): exchange(flux_call(velocity, adj_temp, radial_div), 'row', axis_index_gro...  27.2 us
    all_to_all x1, blocking collectives, body(): pieces = exchange(pieces, 'col', axis_index_groups=col_order)  24.5 us
    all_to_all x1, starting transfers between devices, body(): exchange(flux_call(velocity, adj_temp, radial_div), 'row', axis_index_gro...  6.37 us
    pallas_call x1, Pallas kernels, flux_call(): pl.pallas_call(flux_kernel, grid=(nt // step,), in_specs=[pl.BlockSpec((3...  4.65 us
    unnamed x17, local copies, waits for them, and re-layouts  3.97 us
    pallas_call x1, Pallas kernels, whole_call(): pl.pallas_call(whole_kernel, in_specs=[vmem()] * 7, out_specs=vmem(), out...  3.01 us
  transfers between devices with their start and end apart: 2, of which 1 were waited for; matrix products, arithmetic and copies ran while one was open for 7% of the time, Pallas kernels for 2%

profile of v7, /device:TPU:1, one launch (start us, length us, event | category | flops | bytes accessed | tf_op | source)
XLA Modules:
  0.0 137.5 jit_solution(8103419698075951877)
XLA Ops:
  0.0 0.0 copy-start
  0.0 4.7 %flux.1 = bf16[8,3,2,8,32,128]{5,4,3,2,1,0:T(8,128)(2,1)} custom-call(bf16[3,64,32,256]{3,2,1,0:T(8,128)(2,1)} %v_ref.1, bf16[64,32,256]{2,1,0:T(8,128)(2,1)} %t_ref.1, bf16[256,256]{1,0:T(8,128)(2,1)} %d_ref.1), custom_call_target="tpu_custom_call" | custom-call | tf_op jit(solution)/shard_map/flux/pallas_call | solution.py:57
  4.7 6.4 %all-to-all-start = ((bf16[8,3,2,8,32,128]{5,4,3,2,1,0:T(8,128)(2,1)}), bf16[8,3,2,8,32,128]{5,4,3,2,1,0:T(8,128)(2,1)S(1)}, u32[]{:S(2)}, u32[]{:S(2)}) async-start(bf16[8,3,2,8,32,128]{5,4,3,2,1,0:T(8,128)(2,1)} %flux.1), calls=%async_computation | async-start | bytes 6291456 | tf_op jit(solution)/shard_map/all_to_all | solution.py:291
  11.0 3.9 %copy.10 = bf16[1024,1024]{0,1:T(8,128)(2,1)} copy(bf16[1024,1024]{1,0:T(8,128)(2,1)} %b_ref.1) | data formatting | bytes 4194304 | tf_op args[7]
  15.0 0.0 copy-done
  15.0 0.1 dynamic-slice_bitcast_fusion.2.recip_ref
  15.0 0.7 constant_dynamic-slice_fusion
  15.8 1.7 %dynamic-slice_bitcast_fusion = (bf16[256,256]{1,0:T(8,128)(2,1)}, bf16[256,256]{1,0:T(8,128)(2,1)}) fusion(bf16[21,256,256]{2,1,0:T(8,128)(2,1)} %param.13, s32[]{:T(128)S(6)} %select_n.48, s32[]{:T(128)S(6)} %select_n.46), kind=kLoop, calls=%fused_computation.12 | loop fusion | bytes 524296 | tf_op jit(solution)/shard_map/jit(dynamic_index_in_dim)/squeeze | solution.py:296
  17.5 1.4 %multiply_convert_fusion = (bf16[168,512]{1,0:T(8,128)(2,1)S(1)}, bf16[168,512]{1,0:T(8,128)(2,1)S(1)}) fusion(), kind=kLoop, calls=%fused_computation.7 | loop fusion | flops 1634304 | bytes 344064 | tf_op jit(solution)/shard_map/convert.1
  18.9 2.3 %constant_dynamic-slice_fusion.2 = bf16[32,1,16,1024]{3,2,1,0:T(8,128)(2,1)} fusion(bf16[32,2,16,1024]{3,2,1,0:T(8,128)(2,1)} %bitcast.19, s32[]{:T(128)S(6)} %select_n.44), kind=kLoop, calls=%fused_computation.16 | loop fusion | bytes 2097156 | tf_op jit(solution)/shard_map/dynamic-slice
  21.3 27.2 %all-to-all-done.x_ref = bf16[8,3,2,8,32,128]{5,4,3,2,1,0:T(8,128)(2,1)S(1)} async-done(((bf16[8,3,2,8,32,128]{5,4,3,2,1,0:T(8,128)(2,1)}), bf16[8,3,2,8,32,128]{5,4,3,2,1,0:T(8,128)(2,1)S(1)}, u32[]{:S(2)}, u32[]{:S(2)}) %all-to-all-start) | async-done | bytes 3145760 | tf_op jit(solution)/shard_map/all_to_all | solution.py:291
  48.4 0.0 copy-start.4
  48.4 1.9 %spectra.1 = bf16[16,2,8,24,128]{4,3,2,1,0:T(8,128)(2,1)S(1)} custom-call(bf16[8,3,2,8,32,128]{5,4,3,2,1,0:T(8,128)(2,1)S(1)} %all-to-all-done.x_ref, bf16[336,512]{1,0:T(8,128)(2,1)S(1)} %pad_maximum_fusion.w_ref, f32[1,128]{1,0:T(1,128)S(1)} %dynamic-slice_bitcast_fusion.2.recip_ref), custom_call_target="tpu_custom_call" | custom-call | tf_op jit(solution)/shard_map/spectra/pallas_call | solution.py:123
  50.4 0.0 copy-start.1
  50.4 0.0 copy-start.2
  50.4 55.7 %all_to_all.15 = bf16[256,24,128]{2,1,0:T(8,128)(2,1)S(1)} all-to-all(bf16[256,24,128]{2,1,0:T(8,128)(2,1)S(1)} %bitcast.18), channel_id=1, replica_groups=mesh['row'=8,'col'=32] {'col','row'}, dimensions={0} | all-to-all | bytes 3145728 | tf_op jit(solution)/shard_map/all_to_all | solution.py:313
  106.1 0.1 slice.4.own_ref
  106.2 0.1 collective-permute-start
  106.3 0.0 copy-done.4
  106.3 0.0 copy-done.6
  106.3 0.0 copy-done.7
  106.3 0.0 copy-done.1
  106.3 0.0 copy-done.2
  106.3 0.0 copy-start.3
  106.3 0.0 copy-start.5
  106.3 3.0 %whole_pair.1.whole_ref = bf16[32,32,256]{2,1,0:T(8,128)(2,1)S(1)} custom-call(bf16[32,8,24,128]{3,2,1,0:T(8,128)(2,1)S(1)} %bitcast.23, bf16[1024,1024]{1,0:T(8,128)(2,1)S(1)} %copy-done.4, bf16[1024,1024]{1,0:T(8,128)(2,1)S(1)} %bitcast.16, bf16[1024,1024]{1,0:T(8,128)(2,1)S(1)} %copy-done.2, bf16[256,256]{1,0:T(8,128)(2,1)S(1)} %copy-done.6, ...), custom_call_target="tpu_custom_call" | custom-call | flops 4000000000 | bytes 8000000 | tf_op jit(solution)/shard_map/whole_pair/pallas_call | solution.py:221
  109.3 0.0 collective-permute-done.other_ref
  109.4 0.0 copy-done.3
  109.4 0.0 copy-done.5
  109.4 2.4 %shared_pair.1 = bf16[32,48,256]{2,1,0:T(8,128)(2,1)S(1)} custom-call(s32[1]{0:T(128)} %bitcast.core_ref, bf16[32,8,8,128]{3,2,1,0:T(8,128)(2,1)S(1)} %slice.4.own_ref, bf16[32,8,8,128]{3,2,1,0:T(8,128)(2,1)S(1)} %collective-permute-done.other_ref, bf16[32,32,256]{2,1,0:T(8,128)(2,1)S(1)} %whole_pair.1.whole_ref, bf16[1024,1024]{1,0:T(8,128)(2,1)S(1)} %copy-done.4, ...), custom_call_target="tpu_custom_call" | custom-call | tf_op jit(solution)/shard_map/shared_pair/pallas_call | solution.py:234
  111.8 24.5 %all_to_all.16 = bf16[32,48,256]{2,1,0:T(8,128)(2,1)S(1)} all-to-all(bf16[32,48,256]{2,1,0:T(8,128)(2,1)S(1)} %shared_pair.1), channel_id=1, replica_groups={{0,1,8,9,16,17,24,25,2,3,10,11,18,19,26,27,4,5,12,13,20,21,28,29,6,7,14..., dimensions={0} | all-to-all | bytes 1572864 | tf_op jit(solution)/shard_map/all_to_all | solution.py:325
  136.3 1.2 result.1
  (3 shorter events, 0.0 us)
Async XLA Ops:
  0.0 15.0 %copy-start = (f32[256]{0:T(256)S(1)}, f32[256]{0:T(256)}, u32[]{:S(2)}) copy-start(f32[256]{0:T(256)} %param.12) | copy-start | bytes 3076
  4.7 43.8 %all-to-all-start = ((bf16[8,3,2,8,32,128]{5,4,3,2,1,0:T(8,128)(2,1)}), bf16[8,3,2,8,32,128]{5,4,3,2,1,0:T(8,128)(2,1)S(1)}, u32[]{:S(2)}, u32[]{:S(2)}) async-start(bf16[8,3,2,8,32,128]{5,4,3,2,1,0:T(8,128)(2,1)} %flux.1), calls=%async_computation | async-start | bytes 6291456 | tf_op jit(solution)/shard_map/all_to_all | solution.py:291
  48.4 57.9 %copy-start.4 = (bf16[1024,1024]{1,0:T(8,128)(2,1)S(1)}, bf16[1024,1024]{1,0:T(8,128)(2,1)}, u32[]{:S(2)}) copy-start(bf16[1024,1024]{1,0:T(8,128)(2,1)} %a_ref.3) | copy-start | bytes 6291460
  48.4 57.9 %copy-start.6 = (bf16[256,256]{1,0:T(8,128)(2,1)S(1)}, bf16[256,256]{1,0:T(8,128)(2,1)}, u32[]{:S(2)}) copy-start(bf16[256,256]{1,0:T(8,128)(2,1)} %get-tuple-element.14.r_ref) | copy-start | bytes 393220
  48.4 57.9 %copy-start.7 = (f32[1024]{0:T(1024)S(1)}, f32[1024]{0:T(1024)}, u32[]{:S(2)}) copy-start(f32[1024]{0:T(1024)} %param.17) | copy-start | bytes 12292
  50.4 55.9 %copy-start.1 = (bf16[1024,1024]{0,1:T(8,128)(2,1)S(1)}, bf16[1024,1024]{0,1:T(8,128)(2,1)}, u32[]{:S(2)}) copy-start(bf16[1024,1024]{0,1:T(8,128)(2,1)} %copy.10) | copy-start | bytes 6291460
  50.4 55.9 %copy-start.2 = (bf16[1024,1024]{1,0:T(8,128)(2,1)S(1)}, bf16[1024,1024]{1,0:T(8,128)(2,1)}, u32[]{:S(2)}) copy-start(bf16[1024,1024]{1,0:T(8,128)(2,1)} %b_ref.1) | copy-start | bytes 6291460
  106.2 3.2 %collective-permute-start = (bf16[32,8,8,128]{3,2,1,0:T(8,128)(2,1)S(1)}, bf16[32,8,8,128]{3,2,1,0:T(8,128)(2,1)S(1)}, u32[]{:S(2)}, u32[]{:S(2)}) collective-permute-start(bf16[32,8,8,128]{3,2,1,0:T(8,128)(2,1)S(1)} %slice.4.own_ref), channel_id=1, source_target_pairs={{0,1},{1,0},{2,3},{3,2},{4,5},{5,4},{6,7},{7,6},{8,9},{9,8},{10,11... | collective-permute-start | bytes 1572872 | tf_op jit(solution)/shard_map/ppermute | solution.py:317
  106.3 3.0 %copy-start.3 = (bf16[32,1,16,1024]{3,2,1,0:T(8,128)(2,1)S(1)}, bf16[32,1,16,1024]{3,2,1,0:T(8,128)(2,1)}, u32[]{:S(2)}) copy-start(bf16[32,1,16,1024]{3,2,1,0:T(8,128)(2,1)} %constant_dynamic-slice_fusion.2) | copy-start | bytes 3145732
  106.3 3.0 %copy-start.5 = (bf16[256,256]{1,0:T(8,128)(2,1)S(1)}, bf16[256,256]{1,0:T(8,128)(2,1)}, u32[]{:S(2)}) copy-start(bf16[256,256]{1,0:T(8,128)(2,1)} %get-tuple-element.17.r_ref) | copy-start | bytes 393220
